TPU v7x, 32 devices: a whole 2x2x4 slice. The times are simulated.
32 devices in a mesh: seq: 8 (over y, x, core), head: 4 (over z).
Axes of the slice: x: 2, y: 2, z: 4, core: 2. Of those that a mesh axis runs over, the one named last changes fastest.
Arguments:
- queries: bfloat16 [4096, 512], P('seq', 'head'), may hold values from -6 to 6
- key_rows: bfloat16 [4096, 512], P('seq', 'head'), may hold values from -6 to 6
- value_rows: bfloat16 [4096, 512], P('seq', 'head'), may hold values from -6 to 6
- upstream: bfloat16 [4096, 512], P('seq', 'head'), may hold values from -6 to 6
- exit_weight: bfloat16 [512], P('head'), may hold values from -4 to 4
- labels: int32 [4096], P('seq'), may hold values 0 or 1
- rand_blocks: int32 [64, 3], replicated, may hold values from 0 to 63, as said below
- glob_blocks: int32 [2], replicated, may hold values from 0 to 63, as said below
Outputs:
- attended: bfloat16 [4096, 512], P('seq', 'head')
- token_loss: float32 [4096], P('seq')
- grad_query: float32 [4096, 512], P('seq', 'head')
- grad_key: float32 [4096, 512], P('seq', 'head')
- grad_value: float32 [4096, 512], P('seq', 'head')
Inputs may be any that keep to these rules, and one draw needn't show every extreme that they name: `rand_blocks`: among the 24 entries of the rows of one device (aligned groups of 8 rows), at most 3 lie in any one aligned range of 8 key blocks, and some range holds exactly 3. `glob_blocks`: 2 distinct blocks, the same for every query block; the document's last block is always among them.
All inputs are finite; a program needn't handle non-finite values. No bound on the sum of `labels` on one device may be relied on, other than what follows from the above.
Results may differ from a plain program's by a relative error of at most 0.018.
Values may be sent and summed in bfloat16 or wider, within the bound.
A program may use at most 64 MiB of HBM per device.

v0:
```python
import math

import jax
import jax.numpy as jnp
from jax import lax
from jax.sharding import PartitionSpec as P

BLOCK = 64
RAND = 3
GLOBAL = 2


def spread(x, axis, root):
    mine = lax.axis_index(axis) == root
    return lax.psum(jnp.where(mine, x, jnp.zeros_like(x)), axis)


def slot_tables(rand_blocks, blocks, shards):
    requests = rand_blocks.reshape(shards, blocks * RAND)
    starts = jnp.arange(shards, dtype=jnp.int32) * blocks
    total_blocks = blocks * shards
    behind = (starts - 1) % total_blocks
    beyond = (starts + blocks) % total_blocks
    requests = jnp.concatenate([requests, behind[:, None], beyond[:, None]], axis=1)
    owners = requests // blocks
    offsets = requests % blocks
    onehot = (owners[:, :, None] == jnp.arange(shards, dtype=jnp.int32)[None, None, :]).astype(
        jnp.int32
    )
    ranking = jnp.sum(onehot * jnp.cumsum(onehot, axis=1), axis=2) - 1
    return (owners, offsets, ranking)


def body(queries, key_rows, value_rows, upstream, exit_weight, labels, rand_blocks, glob_blocks):
    tokens, head_dim = queries.shape
    blocks = tokens // BLOCK
    shards = lax.axis_size("seq")
    myself = lax.axis_index("seq")
    total_blocks = blocks * shards
    kv_width = 2 * head_dim
    slot_count = 3 + RAND + GLOBAL
    inv_sqrt = 1.0 / math.sqrt(head_dim)
    rand_dev = blocks * RAND
    packed = jnp.concatenate([key_rows, value_rows], axis=1)
    local_kv = packed.reshape(blocks, BLOCK, kv_width)
    cap_rand = max(1, (rand_dev + shards - 1) // shards)
    capacity = cap_rand + 1
    owners, offsets, ranking = slot_tables(rand_blocks, blocks, shards)
    picked = (owners == myself)[:, :, None] & (
        ranking[:, :, None] == jnp.arange(capacity, dtype=jnp.int32)[None, None, :]
    )
    send_index = jnp.sum(jnp.where(picked, offsets[:, :, None], 0), axis=1)
    slot_used = jnp.any(picked, axis=1)
    outgoing = local_kv[send_index]
    incoming = lax.all_to_all(outgoing, "seq", split_axis=0, concat_axis=0, tiled=True)
    my_owner = lax.dynamic_index_in_dim(owners, myself, 0, keepdims=False)
    my_rank = lax.dynamic_index_in_dim(ranking, myself, 0, keepdims=False)
    slot_row = my_owner * capacity + my_rank
    fetched = incoming.reshape(shards * capacity, BLOCK, kv_width)[slot_row]
    randoms = fetched[:rand_dev].reshape(blocks, RAND, BLOCK, kv_width)
    extended = jnp.concatenate(
        [fetched[rand_dev][None], local_kv, fetched[rand_dev + 1][None]], axis=0
    )
    owner_glob = glob_blocks // blocks
    offset_glob = glob_blocks % blocks
    pieces = []
    for glob_no in range(GLOBAL):
        glob_piece = lax.dynamic_index_in_dim(local_kv, offset_glob[glob_no], 0, keepdims=False)
        pieces.append(spread(glob_piece, "seq", owner_glob[glob_no]))
    shared = jnp.stack(pieces)
    window = jnp.stack([extended[:blocks], extended[1 : blocks + 1], extended[2:]], axis=1)
    gathered_keys = jnp.concatenate(
        [window, randoms, jnp.broadcast_to(shared[None], (blocks, GLOBAL, BLOCK, kv_width))], axis=1
    )
    gathered_keys = gathered_keys.reshape(blocks, slot_count * BLOCK, kv_width)
    key_portion = gathered_keys[..., :head_dim]
    value_portion = gathered_keys[..., head_dim:]
    blocked_queries = queries.reshape(blocks, BLOCK, head_dim)
    block_ids = myself * blocks + jnp.arange(blocks, dtype=jnp.int32)
    slot_ok = jnp.concatenate(
        [
            (block_ids > 0)[:, None],
            jnp.ones((blocks, 1), bool),
            (block_ids < total_blocks - 1)[:, None],
            jnp.ones((blocks, RAND + GLOBAL), bool),
        ],
        axis=1,
    )
    key_ok = jnp.repeat(slot_ok, BLOCK, axis=1)
    attention_scores = (
        jnp.einsum("afs,ans->afn", blocked_queries, key_portion, preferred_element_type=jnp.float32)
        * inv_sqrt
    )
    attention_scores = jnp.where(key_ok[:, None, :], attention_scores, -jnp.inf)
    row_peak = jnp.max(attention_scores, axis=-1, keepdims=True)
    exp_terms = jnp.exp(attention_scores - row_peak)
    probs = exp_terms / jnp.sum(exp_terms, axis=-1, keepdims=True)
    reduced_probabilities = probs.astype(jnp.bfloat16)
    attended = (
        jnp.einsum(
            "omc,och->omh", reduced_probabilities, value_portion, preferred_element_type=jnp.float32
        )
        .astype(jnp.bfloat16)
        .reshape(tokens, head_dim)
    )
    partial_logit = jnp.dot(attended, exit_weight, preferred_element_type=jnp.float32)
    logits = lax.psum(partial_logit, "head")
    target = labels.astype(jnp.float32)
    token_loss = jax.nn.softplus(logits) - target * logits
    dlogits = jax.nn.sigmoid(logits) - target
    grad_out = (
        upstream.astype(jnp.float32) + dlogits[:, None] * exit_weight.astype(jnp.float32)[None, :]
    ).astype(jnp.bfloat16)
    block_gradient = grad_out.reshape(blocks, BLOCK, head_dim)
    probability_gradient = jnp.einsum(
        "afs,ans->afn", block_gradient, value_portion, preferred_element_type=jnp.float32
    )
    row_dot = jnp.sum(probs * probability_gradient, axis=-1, keepdims=True)
    score_gradient = (probs * (probability_gradient - row_dot) * inv_sqrt).astype(jnp.bfloat16)
    grad_query = jnp.einsum(
        "omc,och->omh", score_gradient, key_portion, preferred_element_type=jnp.float32
    ).reshape(tokens, head_dim)
    key_gradient = jnp.einsum(
        "tnc,tny->tcy", score_gradient, blocked_queries, preferred_element_type=jnp.float32
    )
    value_gradient = jnp.einsum(
        "tnc,tny->tcy", reduced_probabilities, block_gradient, preferred_element_type=jnp.float32
    )
    slot_grads = jnp.concatenate([key_gradient, value_gradient], axis=-1).reshape(
        blocks, slot_count, BLOCK, kv_width
    )
    to_prev = slot_grads[:, 0].astype(jnp.bfloat16)
    to_next = slot_grads[:, 2].astype(jnp.bfloat16)
    rand_grads = slot_grads[:, 3 : 3 + RAND].astype(jnp.bfloat16).reshape(rand_dev, BLOCK, kv_width)
    zero_block = jnp.zeros((1, BLOCK, kv_width), jnp.float32)
    kv_total = slot_grads[:, 1] + jnp.concatenate(
        [to_prev[1:].astype(jnp.float32), zero_block], axis=0
    )
    kv_total = kv_total + jnp.concatenate([zero_block, to_next[:-1].astype(jnp.float32)], axis=0)
    entries = jnp.concatenate([rand_grads, to_prev[:1], to_next[-1:]], axis=0)
    placing = (slot_row[None, :] == jnp.arange(shards * capacity, dtype=jnp.int32)[:, None]).astype(
        jnp.bfloat16
    )
    outgoing_grads = jnp.einsum(
        "se,exf->sxf", placing, entries, preferred_element_type=jnp.float32
    ).astype(jnp.bfloat16)
    outgoing_grads = outgoing_grads.reshape(shards, capacity, BLOCK, kv_width)
    returned = lax.all_to_all(
        outgoing_grads, "seq", split_axis=0, concat_axis=0, tiled=True
    ).reshape(shards * capacity, BLOCK, kv_width)
    receive_map = (
        (send_index.reshape(-1)[None, :] == jnp.arange(blocks, dtype=jnp.int32)[:, None])
        & slot_used.reshape(-1)[None, :]
    ).astype(jnp.bfloat16)
    kv_total = kv_total + jnp.einsum(
        "bs,sxf->bxf", receive_map, returned, preferred_element_type=jnp.float32
    )
    glob_terms = jnp.sum(slot_grads[:, 3 + RAND :], axis=0)
    glob_total = lax.psum(glob_terms.astype(jnp.bfloat16), "seq").astype(jnp.float32)
    for glob_no in range(GLOBAL):
        is_home = (owner_glob[glob_no] == myself) & (
            jnp.arange(blocks, dtype=jnp.int32) == offset_glob[glob_no]
        )
        kv_total = kv_total + jnp.where(is_home[:, None, None], glob_total[glob_no][None], 0.0)
    grad_key = kv_total[..., :head_dim].reshape(tokens, head_dim)
    grad_value = kv_total[..., head_dim:].reshape(tokens, head_dim)
    return (attended, token_loss, grad_query, grad_key, grad_value)


def solution(mesh):
    placed = (
        P("seq", "head"),
        P("seq", "head"),
        P("seq", "head"),
        P("seq", "head"),
        P("head"),
        P("seq"),
        P(),
        P(),
    )
    return jax.shard_map(
        body,
        mesh=mesh,
        in_specs=placed,
        out_specs=(
            P("seq", "head"),
            P("seq"),
            P("seq", "head"),
            P("seq", "head"),
            P("seq", "head"),
        ),
        check_vma=False,
    )
```

profile of v0, /device:TPU:0, one launch (start us, length us, event | category | flops | bytes accessed | tf_op | source)
XLA Modules:
  0.0 201.8 jit_solution(10489605091353121662)
XLA Ops:
  9.4 0.9 constant_dynamic-update-slice_fusion.1
  10.3 0.9 constant_dynamic-update-slice_fusion
  11.3 1.6 gather_fusion
  12.9 5.2 %all-to-all-start = ((bf16[8,4,64,256]{3,2,1,0:T(8,128)(2,1)}), bf16[8,4,64,256]{3,2,1,0:T(8,128)(2,1)S(1)}, u32[]{:S(2)}, u32[]{:S(2)}) async-start(bf16[8,4,64,256]{3,2,1,0:T(8,128)(2,1)} %bitcast.2), calls=%async_computation | async-start | bytes 2097152 | tf_op jit(solution)/shard_map/all_to_all | solution.py:55
  26.8 52.0 %all-reduce.8.cloned.1.call-done = (bf16[1,64,256]{2,1,0:T(8,128)(2,1)}, bf16[1,64,256]{2,1,0:T(8,128)(2,1)}) async-done(((bf16[1,64,256]{2,1,0:T(8,128)(2,1)}, bf16[1,64,256]{2,1,0:T(8,128)(2,1)}), (bf16[1,64,256]{2,1,0:T(8,128)(2,1)}, bf16[1,64,256]{2,1,0:T(8,128)(2,1)})) %all-reduce.8.cloned.1.call-update) | async-done | bytes 65552 | tf_op jit(solution)/shard_map/psum | solution.py:15
  81.0 1.5 fusion.74
  82.5 2.6 %convolution_convert_fusion.1 = bf16[8,64,128]{2,1,0:T(8,128)(2,1)S(1)} fusion(bf16[8,512,256]{2,1,0:T(8,128)(2,1)} %bitcast.101, f32[8,64]{1,0:T(8,128)S(1)} %get-tuple-element.31, f32[8,64,512]{2,1,0:T(8,128)S(1)} %fusion.8), kind=kOutput, calls=%fused_computation.18 | convolution fusion | flops 67961856 | bytes 3280896 | tf_op jit(solution)/shard_map/omc,och->omh/dot_general | solution.py:100
  85.3 11.7 %psum.30 = f32[512]{0:T(512)S(1)} all-reduce(f32[512]{0:T(512)S(1)} %bitcast.110), channel_id=1, replica_groups=mesh['seq'=8,'head'=4] {'head'}, use_global_device_ids=true, to_apply=%region_7.8 | all-reduce | flops 512 | bytes 4096 | tf_op jit(solution)/shard_map/psum | solution.py:107
  97.7 2.7 %fusion.23 = f32[8,64,512]{2,1,0:T(8,128)} fusion(bf16[8,64,128]{2,1,0:T(8,128)(2,1)S(1)} %bitcast.104, bf16[8,512,256]{2,1,0:T(8,128)(2,1)} %bitcast.102), kind=kOutput, calls=%fused_computation.31 | convolution fusion | flops 67108864 | bytes 2228224 | tf_op jit(solution)/shard_map/afs,ans->afn/dot_general | solution.py:115
  100.4 2.7 %fusion.36 = f32[8,512,128]{1,2,0:T(8,128)S(1)} fusion(bf16[8,64,128]{2,1,0:T(8,128)(2,1)S(1)} %bitcast.105, f32[8,64]{1,0:T(8,128)S(1)} %get-tuple-element.31, f32[8,64,512]{2,1,0:T(8,128)} %copy-done.2), kind=kOutput, calls=%fused_computation.51 | convolution fusion | flops 67896320 | bytes 3278848 | tf_op jit(solution)/shard_map/tnc,tny->tcy/dot_general | solution.py:126
  103.1 5.6 %fusion.17 = f32[8,512,128]{1,2,0:T(8,128)} fusion(bf16[8,64,128]{2,1,0:T(8,128)(2,1)S(1)} %bitcast.88, f32[8,64,512]{2,1,0:T(8,128)} %fusion.23, f32[8,64,512]{2,1,0:T(8,128)S(1)} %get-tuple-element.32, f32[8,64]{1,0:T(8,128)S(1)} %get-tuple-element.31), kind=kOutput, calls=%fused_computation.26 | convolution fusion | flops 68944896 | bytes 4327424 | tf_op jit(solution)/shard_map/tnc,tny->tcy/dot_general | solution.py:123
  108.7 4.2 %pad_maximum_fusion = f32[8,512,256]{1,2,0:T(8,128)} fusion(f32[8,512,128]{1,2,0:T(8,128)S(1)} %fusion.36, f32[8,512,128]{1,2,0:T(8,128)} %fusion.17), kind=kLoop, calls=%fused_computation.4 | loop fusion | flops 1048576 | bytes 8388608 | tf_op jit(solution)/shard_map/concatenate | solution.py:129
  112.9 5.4 %copy.173 = f32[8,512,256]{2,0,1:T(8,128)} copy(f32[8,512,256]{1,2,0:T(8,128)} %pad_maximum_fusion) | data formatting | bytes 8388608 | tf_op jit(solution)/shard_map/reshape | solution.py:129
  118.4 2.4 %convert.11 = bf16[8,8,64,256]{3,0,2,1:T(8,128)(2,1)S(1)} convert(f32[8,8,64,256]{3,0,2,1:T(8,128)} %bitcast.89) | non-fusion elementwise | flops 1048576 | bytes 6291456 | tf_op jit(solution)/shard_map/convert.8
  121.6 1.5 convolution_convert_fusion
  123.1 1.3 reshape.419
  124.4 1.4 copy.169
  125.8 3.6 %all-to-all-start.1 = ((bf16[8,4,64,256]{3,1,2,0:T(4,128)(2,1)}), bf16[8,4,64,256]{3,1,2,0:T(4,128)(2,1)S(1)}, u32[]{:S(2)}, u32[]{:S(2)}) async-start(bf16[8,4,64,256]{3,1,2,0:T(4,128)(2,1)} %copy.169), calls=%async_computation.1 | async-start | bytes 2097152 | tf_op jit(solution)/shard_map/all_to_all | solution.py:148
  130.4 5.3 %copy.160 = f32[8,512,256]{2,1,0:T(8,128)} copy(f32[8,512,256]{1,2,0:T(8,128)} %pad_maximum_fusion) | data formatting | bytes 8388608 | tf_op jit(solution)/shard_map/concatenate | solution.py:129
  135.8 1.9 slice_reduce_fusion
  137.7 5.7 %fusion.18 = f32[8,64,128]{2,1,0:T(8,128)} fusion(f32[8,64,512]{2,1,0:T(8,128)} %fusion.23, bf16[8,512,256]{2,1,0:T(8,128)(2,1)} %bitcast.103, f32[8,64,512]{2,1,0:T(8,128)} %copy-done.1, f32[8,64]{1,0:T(8,128)S(1)} %get-tuple-element.31), kind=kOutput, calls=%fused_computation.27 | convolution fusion | flops 68944896 | bytes 5513216 | tf_op jit(solution)/shard_map/omc,och->omh/dot_general | solution.py:120
  144.2 44.7 %all-reduce.6.cloned.1.call-done = bf16[2,64,256]{2,1,0:T(8,128)(2,1)} async-done(((bf16[2,64,256]{2,1,0:T(8,128)(2,1)}), bf16[2,64,256]{2,1,0:T(8,128)(2,1)}) %all-reduce.6.cloned.1.call-update) | async-done | bytes 65552 | tf_op jit(solution)/shard_map/psum | solution.py:159
  189.0 0.8 convert_element_type.60
  191.9 1.5 fusion.11
  (86 shorter events, 13.8 us)
Async XLA Ops:
  7.2 73.3 %copy-start = (bf16[512,128]{1,0:T(8,128)(2,1)S(1)}, bf16[512,128]{1,0:T(8,128)(2,1)}, u32[]{:S(2)}) copy-start(bf16[512,128]{1,0:T(8,128)(2,1)} %param.8) | copy-start | bytes 393220
  11.2 6.8 %copy-start.10 = (s32[2]{0:T(128)S(1)}, s32[2]{0:T(128)}, u32[]{:S(2)}) copy-start(s32[2]{0:T(128)} %param.15) | copy-start | bytes 28
  11.3 15.4 %copy-start.9 = (bf16[128]{0:T(256)(128)(2,1)S(1)}, bf16[128]{0:T(256)(128)(2,1)}, u32[]{:S(2)}) copy-start(bf16[128]{0:T(256)(128)(2,1)} %param.12) | copy-start | bytes 772
  12.9 66.7 %all-to-all-start = ((bf16[8,4,64,256]{3,2,1,0:T(8,128)(2,1)}), bf16[8,4,64,256]{3,2,1,0:T(8,128)(2,1)S(1)}, u32[]{:S(2)}, u32[]{:S(2)}) async-start(bf16[8,4,64,256]{3,2,1,0:T(8,128)(2,1)} %bitcast.2), calls=%async_computation | async-start | bytes 2097152 | tf_op jit(solution)/shard_map/all_to_all | solution.py:55
  18.0 60.7 %all-reduce.8.cloned.1.call-start = ((), (), s32[]{:S(2)}) async-start(), calls=%async_computation.3 | async-start | bytes 131072 | tf_op jit(solution)/shard_map/psum | solution.py:15
  80.5 2.0 copy-start.3
  81.0 4.2 %copy-start.2 = (f32[8,64,512]{2,1,0:T(8,128)}, f32[8,64,512]{2,1,0:T(8,128)S(1)}, u32[]{:S(2)}) copy-start(f32[8,64,512]{2,1,0:T(8,128)S(1)} %fusion.8) | copy-start | bytes 3145732
  82.5 20.6 %copy-start.1 = (f32[8,64,512]{2,1,0:T(8,128)}, f32[8,64,512]{2,1,0:T(8,128)S(1)}, u32[]{:S(2)}) copy-start(f32[8,64,512]{2,1,0:T(8,128)S(1)} %get-tuple-element.32) | copy-start | bytes 3145732
  82.5 14.5 %copy-start.8 = (s32[512]{0:T(512)S(1)}, s32[512]{0:T(512)}, u32[]{:S(2)}) copy-start(s32[512]{0:T(512)} %param.13) | copy-start | bytes 6148
  82.5 15.1 %copy-start.6 = (bf16[512,128]{1,0:T(8,128)(2,1)S(1)}, bf16[512,128]{1,0:T(8,128)(2,1)}, u32[]{:S(2)}) copy-start(bf16[512,128]{1,0:T(8,128)(2,1)} %param.11) | copy-start | bytes 393220
  85.1 12.6 %copy-start.7 = (bf16[8,64,128]{2,1,0:T(8,128)(2,1)}, bf16[8,64,128]{2,1,0:T(8,128)(2,1)S(1)}, u32[]{:S(2)}) copy-start(bf16[8,64,128]{2,1,0:T(8,128)(2,1)S(1)} %convolution_convert_fusion.1) | copy-start | bytes 393220
  125.8 64.7 %all-to-all-start.1 = ((bf16[8,4,64,256]{3,1,2,0:T(4,128)(2,1)}), bf16[8,4,64,256]{3,1,2,0:T(4,128)(2,1)S(1)}, u32[]{:S(2)}, u32[]{:S(2)}) async-start(bf16[8,4,64,256]{3,1,2,0:T(4,128)(2,1)} %copy.169), calls=%async_computation.1 | async-start | bytes 2097152 | tf_op jit(solution)/shard_map/all_to_all | solution.py:148
  129.4 59.6 %all-reduce.6.cloned.1.call-start = ((), (), s32[]{:S(2)}) async-start(), calls=%async_computation.2 | async-start | bytes 131072 | tf_op jit(solution)/shard_map/psum | solution.py:159
  191.1 0.8 copy-start.4
  191.1 0.9 copy-start.5
Sparse Core Ops, SparseCore 0:
  24.4 54.2 all-reduce.7
  137.9 51.0 all-reduce.5
where the time goes:
time: 203 us; the launch traced here: 202 us
  waiting for transfers between devices  96.7 us (48%)
  local copies, waits for them, and re-layouts  25.5 us (13%)
  matrix products  22.9 us (11%)
  between operations  20.7 us (10%)
  other arithmetic  15.5 us (8%)
  blocking collectives  11.7 us (6%)
  starting transfers between devices  8.8 us (4%)
    psum x1, waiting for transfers between devices, spread(): return lax.psum(jnp.where(mine, x, jnp.zeros_like(x)), axis)  52 us
    psum x1, waiting for transfers between devices, body(): lax.psum(glob_terms.astype(jnp.bfloat16), 'seq').astype(jnp.float32)  44.7 us
    psum x1, blocking collectives, body(): logits = lax.psum(partial_logit, 'head')  11.7 us
    dot_general x1, matrix products, body(): jnp.einsum('omc,och->omh', score_gradient, key_portion, preferred_element...  5.75 us
    dot_general x1, matrix products, body(): jnp.einsum('tnc,tny->tcy', score_gradient, blocked_queries, preferred_ele...  5.61 us
    reshape x1, local copies, waits for them, and re-layouts, body(): jnp.concatenate([key_gradient, value_gradient], axis=-1)  5.44 us
    concatenate x1, local copies, waits for them, and re-layouts, body(): jnp.concatenate([key_gradient, value_gradient], axis=-1)  5.35 us
    all_to_all x1, starting transfers between devices, body(): lax.all_to_all(outgoing, 'seq', split_axis=0, concat_axis=0, tiled=True)  5.17 us
  transfers between devices with their start and end apart: 4, of which 2 were waited for; matrix products, arithmetic and copies ran while one was open for 10% of the time, Pallas kernels for 0%

commit v1 on v0

v1 whole, which is shorter than its diff:
```python
import functools
import math

import jax
import jax.numpy as jnp
from jax import lax
from jax.experimental import pallas as pl
from jax.experimental.pallas import tpu as pltpu
from jax.sharding import PartitionSpec as P

BLOCK = 64
RAND = 3
GLOBAL = 2
SLOTS = 3 + RAND + GLOBAL
MESH = pl.DeviceIdType.MESH
F32 = jnp.float32
BF16 = jnp.bfloat16
CONTRACT_LAST = (((1,), (1,)), ((), ()))
CONTRACT_FIRST = (((0,), (0,)), ((), ()))
PARTS = 8


def flip(me, bits):
    out = me
    bit = 1
    while bit <= bits:
        if bits & bit:
            out = out + (1 - 2 * lax.rem(lax.div(me, jnp.int32(bit)), jnp.int32(2))) * bit
        bit *= 2
    return out


def kernel(
    S, H, nb, D, cap,
    q_ref, k_ref, v_ref, up_ref, w_ref, lab_ref, rand_ref, glob_ref,
    att_ref, loss_ref, dq_ref, dk_ref, dv_ref,
    kall, vall, p_s, ds_s, g_s, rg, og, og_in, acc, gacc, gsend, grecv, gsum, gall,
    edge_out, edge_in, lmine, lrecv, sidx, roff,
    ag_send, ag_fwd, ag_recv, l_send, l_recv, o_send, o_recv, e_send, e_recv,
    gp_send, gp_recv, gb_send, gb_recv,
):
    me = lax.axis_index("seq")
    hd = lax.axis_index("head")
    N = S * nb
    inv = 1.0 / math.sqrt(D)
    stride = max(1, S // PARTS)
    rows = GLOBAL * BLOCK // PARTS
    T = nb * BLOCK

    def seq_copy(src, dst, ssem, rsem, peer):
        return pltpu.make_async_remote_copy(
            src_ref=src, dst_ref=dst, send_sem=ssem, recv_sem=rsem,
            device_id={"seq": peer}, device_id_type=MESH)

    barrier = pltpu.get_barrier_semaphore()
    for d in range(1, S):
        pl.semaphore_signal(barrier, inc=1, device_id={"seq": flip(me, d)}, device_id_type=MESH)
    for d in range(1, H):
        pl.semaphore_signal(barrier, inc=1, device_id={"head": lax.rem(hd + d, H)}, device_id_type=MESH)
    pl.semaphore_wait(barrier, S - 1 + H - 1)

    mine = pl.ds(me * nb, nb)
    pairs = ((k_ref, kall), (v_ref, vall))
    evens = [d for d in range(S - 2, 0, -2)]
    partner = flip(me, 1)
    for a, (src, dst) in enumerate(pairs):
        for d in evens + [1]:
            seq_copy(src, dst.at[mine], ag_send.at[a, d], ag_recv.at[a, me], flip(me, d)).start()

    kall[mine] = k_ref[...]
    vall[mine] = v_ref[...]

    def tables(s, carry):
        zero = jnp.int32(0)
        cnt, cnt2 = zero, zero
        idx = [zero] * cap
        off = [jnp.int32(-1)] * cap
        for j in range(nb * RAND):
            b = rand_ref[me * nb + j // RAND, j % RAND]
            hit = lax.div(b, jnp.int32(nb)) == s
            c = rand_ref[s * nb + j // RAND, j % RAND]
            hit2 = lax.div(c, jnp.int32(nb)) == me
            place = lax.rem(c, jnp.int32(nb))
            for t in range(cap):
                idx[t] = jnp.where(hit & (cnt == t), j, idx[t])
                off[t] = jnp.where(hit2 & (cnt2 == t), place, off[t])
            cnt = cnt + hit.astype(jnp.int32)
            cnt2 = cnt2 + hit2.astype(jnp.int32)
        for t in range(cap):
            sidx[s, t] = idx[t]
            roff[s, t] = off[t]
        return carry

    lax.fori_loop(0, S, tables, 0)

    for a, (src, dst) in enumerate(pairs):
        for d in sorted(evens, key=lambda d: bin(d).count("1")):
            owner = flip(me, d)
            part = dst.at[pl.ds(owner * nb, nb)]
            seq_copy(src, part, ag_send.at[a, d], ag_recv.at[a, owner], owner).wait_recv()
            seq_copy(part, part, ag_fwd.at[a, d], ag_recv.at[a, owner], partner).start()
    for a, (src, dst) in enumerate(pairs):
        for d in range(1, S, 2):
            owner = flip(me, d)
            part = dst.at[pl.ds(owner * nb, nb)]
            seq_copy(src, part, ag_send.at[a, d], ag_recv.at[a, owner], owner).wait_recv()

    def gather(all_ref, i):
        gi = me * nb + i
        ids = [lax.rem(gi + N - 1, N), gi, lax.rem(gi + 1, N)]
        ids += [rand_ref[gi, r] for r in range(RAND)]
        ids += [glob_ref[r] for r in range(GLOBAL)]
        return jnp.concatenate([all_ref[b] for b in ids], axis=0)

    col = lax.broadcasted_iota(jnp.int32, (BLOCK, SLOTS * BLOCK), 1)

    def forward(i):
        keys = gather(kall, i)
        s = lax.dot_general(q_ref[i], keys, CONTRACT_LAST, preferred_element_type=F32) * inv
        gi = me * nb + i
        low = jnp.where(gi == 0, BLOCK, 0)
        void = (col < low) | ((col >= 2 * BLOCK) & (col < jnp.where(gi == N - 1, 3 * BLOCK, 0)))
        s = jnp.where(void, -jnp.inf, s)
        e = jnp.exp(s - jnp.max(s, axis=-1, keepdims=True))
        p = e * (1.0 / jnp.sum(e, axis=-1, keepdims=True))
        p_s[i] = p
        o = jnp.dot(p.astype(BF16), gather(vall, i), preferred_element_type=F32)
        att_ref[i] = o.astype(BF16)

    def fwd_pair(t, carry):
        forward(2 * t)
        forward(2 * t + 1)
        return carry

    lax.fori_loop(0, nb // 2, fwd_pair, 0)

    w = w_ref[...]
    part = lax.dot_general(
        jnp.broadcast_to(w, (16, D)), att_ref[...].reshape(T, D), CONTRACT_LAST,
        preferred_element_type=F32)[0:1]
    lmine[...] = part

    def logit_copy(d, slot):
        return pltpu.make_async_remote_copy(
            src_ref=lmine, dst_ref=lrecv.at[slot], send_sem=l_send.at[d], recv_sem=l_recv.at[slot],
            device_id={"head": lax.rem(hd + d, H)}, device_id_type=MESH)

    for d in range(1, H):
        logit_copy(d, hd).start()
    acc[...] = jnp.zeros_like(acc)
    gacc[...] = jnp.zeros_like(gacc)
    logits = part
    for d in range(1, H):
        slot = lax.rem(hd + d, H)
        logit_copy(d, slot).wait_recv()
        logits = logits + lrecv[slot]
    target = lab_ref[...].astype(F32)
    e = jnp.exp(-jnp.abs(logits))
    loss_ref[...] = jnp.maximum(logits, 0.0) + jnp.log1p(e) - target * logits
    sig = jnp.where(logits >= 0, 1.0, e) / (1.0 + e)
    dl = jnp.broadcast_to(sig - target, (8, T)).T[:, 0:1]
    grad_out = up_ref[...].reshape(T, D).astype(F32) + dl * w.astype(F32)
    g_s[...] = grad_out.astype(BF16).reshape(nb, BLOCK, D)

    def backward(i):
        g = g_s[i]
        dp = lax.dot_general(g, gather(vall, i), CONTRACT_LAST, preferred_element_type=F32)
        p = p_s[i]
        rd = jnp.sum(p * dp, axis=-1, keepdims=True)
        ds = (p * (dp - rd) * inv).astype(BF16)
        ds_s[i] = ds
        dk = lax.dot_general(ds, q_ref[i], CONTRACT_FIRST, preferred_element_type=F32)
        dv = lax.dot_general(p.astype(BF16), g, CONTRACT_FIRST, preferred_element_type=F32)
        both = jnp.concatenate([dk, dv], axis=1)
        acc[pl.ds(i, 3)] += both[: 3 * BLOCK].reshape(3, BLOCK, 2 * D)
        rg[pl.ds(i * RAND, RAND)] = (
            both[3 * BLOCK : (3 + RAND) * BLOCK].astype(BF16).reshape(RAND, BLOCK, 2 * D))
        gacc[...] += both[(3 + RAND) * BLOCK :]

    def bwd_pair(t, carry):
        backward(2 * t)
        backward(2 * t + 1)
        return carry

    lax.fori_loop(0, nb // 2, bwd_pair, 0)

    gsend[...] = gacc[...].astype(BF16)
    is_part = lax.rem(me, stride) == 0
    my_part = lax.div(me, jnp.int32(stride))

    def part_copy(j, owner, slot):
        return seq_copy(gsend.at[pl.ds(j * rows, rows)], grecv.at[slot], gp_send.at[j], gp_recv.at[slot], owner)

    for t in range(PARTS):
        j = lax.rem(my_part + t, PARTS)
        owner = j * stride

        @pl.when(owner != me)
        def _():
            part_copy(j, owner, me).start()

    edge_out[0] = acc[0].astype(BF16)
    edge_out[1] = acc[nb + 1].astype(BF16)
    prev, following = lax.rem(me + S - 1, S), lax.rem(me + 1, S)
    to_prev = seq_copy(edge_out.at[0], edge_in.at[1], e_send.at[0], e_recv.at[1], prev)
    to_next = seq_copy(edge_out.at[1], edge_in.at[0], e_send.at[1], e_recv.at[0], following)
    to_prev.start()
    to_next.start()

    order = sorted(range(1, S), key=lambda d: -bin(d // 2).count("1"))

    def out_copy(d, peer, slot):
        return seq_copy(og.at[peer], og_in.at[slot], o_send.at[d], o_recv.at[slot], peer)

    for d in order:
        peer = flip(me, d)
        for t in range(cap):
            og[peer, t] = rg[sidx[peer, t]]
        out_copy(d, peer, me).start()

    def grad_q(i):
        dq_ref[i] = jnp.dot(ds_s[i], gather(kall, i), preferred_element_type=F32)

    def dq_pair(t, carry):
        grad_q(2 * t)
        grad_q(2 * t + 1)
        return carry

    lax.fori_loop(0, nb // 2, dq_pair, 0)

    def take(block, place):
        block = block.astype(F32)
        for b in range(nb):
            acc[1 + b] += block * (place == b).astype(F32)

    for t in range(cap):
        take(rg[sidx[me, t]], roff[me, t])

    def share_copy(d, peer, slot):
        return seq_copy(gsum, gall.at[slot], gb_send.at[d], gb_recv.at[slot], peer)

    @pl.when(is_part)
    def _():
        total = gsend[pl.ds(my_part * rows, rows)].astype(F32)
        for d in range(1, S):
            peer = flip(me, d)
            part_copy(my_part, peer, peer).wait_recv()
            total = total + grecv[peer].astype(F32)
        gsum[...] = total.astype(BF16)
        gall[my_part] = gsum[...]
        for d in range(1, S):
            share_copy(d, flip(me, d), my_part).start()

    for d in sorted(order, key=lambda d: bin(d).count("1")):
        peer = flip(me, d)
        out_copy(d, peer, peer).wait_recv()
        for t in range(cap):
            take(og_in[peer, t], roff[peer, t])

    to_prev.wait_recv()
    to_next.wait_recv()
    acc[1] += edge_in[0].astype(F32)
    acc[nb] += edge_in[1].astype(F32)

    for t in range(PARTS):
        j = lax.rem(my_part + t, PARTS)

        @pl.when(j * stride != me)
        def _():
            share_copy(0, me, j).wait_recv()

    for n in range(GLOBAL):
        count = PARTS // GLOBAL
        block = gall[n * count : (n + 1) * count].astype(F32).reshape(BLOCK, 2 * D)
        take(block, glob_ref[n] - me * nb)

    total = acc[1 : nb + 1]
    dk_ref[...] = total[:, :, :D]
    dv_ref[...] = total[:, :, D:]

    for a, (src, dst) in enumerate(pairs):
        for d in evens + [1]:
            seq_copy(src, dst.at[mine], ag_send.at[a, d], ag_recv.at[a, me], flip(me, d)).wait_send()
        for d in evens:
            part = dst.at[pl.ds(flip(me, d) * nb, nb)]
            seq_copy(part, part, ag_fwd.at[a, d], ag_recv.at[a, me], partner).wait_send()
    for d in range(1, H):
        logit_copy(d, hd).wait_send()
    for t in range(PARTS):
        j = lax.rem(my_part + t, PARTS)
        owner = j * stride

        @pl.when(owner != me)
        def _():
            part_copy(j, owner, me).wait_send()

    to_prev.wait_send()
    to_next.wait_send()
    for d in order:
        peer = flip(me, d)
        out_copy(d, peer, me).wait_send()

    @pl.when(is_part)
    def _():
        for d in range(1, S):
            share_copy(d, flip(me, d), my_part).wait_send()


def body(S, H, queries, key_rows, value_rows, upstream, exit_weight, labels, rand_blocks, glob_blocks):
    T, D = queries.shape
    nb = T // BLOCK
    cap = max(1, (nb * RAND + S - 1) // S)
    W = 2 * D
    rows = GLOBAL * BLOCK // PARTS
    blocked = lambda x: x.reshape(nb, BLOCK, D)
    vmem = pl.BlockSpec(memory_space=pltpu.VMEM)
    smem = pl.BlockSpec(memory_space=pltpu.SMEM)
    dma = pltpu.SemaphoreType.DMA
    att, loss, dq, dk, dv = pl.pallas_call(
        functools.partial(kernel, S, H, nb, D, cap),
        out_shape=(
            jax.ShapeDtypeStruct((nb, BLOCK, D), BF16),
            jax.ShapeDtypeStruct((1, T), F32),
            jax.ShapeDtypeStruct((nb, BLOCK, D), F32),
            jax.ShapeDtypeStruct((nb, BLOCK, D), F32),
            jax.ShapeDtypeStruct((nb, BLOCK, D), F32),
        ),
        in_specs=[vmem] * 6 + [smem] * 2,
        out_specs=[vmem] * 5,
        scratch_shapes=[
            pltpu.VMEM((S * nb, BLOCK, D), BF16),
            pltpu.VMEM((S * nb, BLOCK, D), BF16),
            pltpu.VMEM((nb, BLOCK, SLOTS * BLOCK), F32),
            pltpu.VMEM((nb, BLOCK, SLOTS * BLOCK), BF16),
            pltpu.VMEM((nb, BLOCK, D), BF16),
            pltpu.VMEM((nb * RAND, BLOCK, W), BF16),
            pltpu.VMEM((S, cap, BLOCK, W), BF16),
            pltpu.VMEM((S, cap, BLOCK, W), BF16),
            pltpu.VMEM((nb + 2, BLOCK, W), F32),
            pltpu.VMEM((GLOBAL * BLOCK, W), F32),
            pltpu.VMEM((GLOBAL * BLOCK, W), BF16),
            pltpu.VMEM((S, rows, W), BF16),
            pltpu.VMEM((rows, W), BF16),
            pltpu.VMEM((PARTS, rows, W), BF16),
            pltpu.VMEM((2, BLOCK, W), BF16),
            pltpu.VMEM((2, BLOCK, W), BF16),
            pltpu.VMEM((1, T), F32),
            pltpu.VMEM((H, 1, T), F32),
            pltpu.SMEM((S, cap), jnp.int32),
            pltpu.SMEM((S, cap), jnp.int32),
            dma((2, S)), dma((2, S)), dma((2, S)),
            dma((H,)), dma((H,)),
            dma((S,)), dma((S,)),
            dma((2,)), dma((2,)),
            dma((PARTS,)), dma((S,)),
            dma((S,)), dma((PARTS,)),
        ],
        compiler_params=pltpu.CompilerParams(
            collective_id=0, has_side_effects=True, vmem_limit_bytes=48 * 1024 * 1024),
    )(
        blocked(queries), blocked(key_rows), blocked(value_rows), blocked(upstream),
        exit_weight.reshape(1, D), labels.reshape(1, T), rand_blocks, glob_blocks,
    )
    flat = lambda x: x.reshape(T, D)
    return (flat(att), loss.reshape(T), flat(dq), flat(dk), flat(dv))


def solution(mesh):
    placed = (
        P("seq", "head"),
        P("seq", "head"),
        P("seq", "head"),
        P("seq", "head"),
        P("head"),
        P("seq"),
        P(),
        P(),
    )
    return jax.shard_map(
        functools.partial(body, mesh.shape["seq"], mesh.shape["head"]),
        mesh=mesh,
        in_specs=placed,
        out_specs=(
            P("seq", "head"),
            P("seq"),
            P("seq", "head"),
            P("seq", "head"),
            P("seq", "head"),
        ),
        check_vma=False,
    )
```

time: 203 us -> 54.1 us (0.27)
  waiting for transfers between devices: 96.7 us -> 0 us
  Pallas kernels: 0 us -> 44.9 us
  matrix products: 22.9 us -> 0 us
  between operations: 20.7 us -> 0.66 us
  local copies, waits for them, and re-layouts: 25.5 us -> 8.32 us
  other arithmetic: 15.5 us -> 0 us
  blocking collectives: 11.7 us -> 0 us
  starting transfers between devices: 8.8 us -> 0 us
    psum x2 -> x0, waiting for transfers between devices: 96.7 us -> none  [the longest x1 52 us: spread(): return lax.psum(jnp.where(mine, x, jnp.zeros_like(x)), axis)]
    pallas_call x0 -> x1, Pallas kernels: none -> 44.9 us  [body(): pl.pallas_call(functools.partial(kernel, S, H, nb, D, cap), out_shape=(ja...]
    dot_general x9 -> x0, matrix products: 22.9 us -> none  [the longest x1 5.75 us: body(): jnp.einsum('omc,och->omh', score_gradient, key_portion, preferred_element...]
    psum x1 -> x0, blocking collectives: 11.7 us -> none  [body(): logits = lax.psum(partial_logit, 'head')]
    reshape x5 -> x0, local copies, waits for them, and re-layouts: 8.9 us -> none  [the longest x1 5.44 us: body(): jnp.concatenate([key_gradient, value_gradient], axis=-1)]
    all_to_all x2 -> x0, starting transfers between devices: 8.73 us -> none  [the longest x1 5.17 us: body(): lax.all_to_all(outgoing, 'seq', split_axis=0, concat_axis=0, tiled=True)]
    concatenate x6 -> x0, local copies, waits for them, and re-layouts: 6.56 us -> none  [the longest x1 5.35 us: body(): jnp.concatenate([key_gradient, value_gradient], axis=-1)]
    unnamed x26 -> x22, local copies, waits for them, and re-layouts: 2.45 us -> 8.32 us
  transfers between devices with their start and end apart: 4 -> 0, of which waited for: 2 -> 0; matrix products, arithmetic and copies ran while one was open for 10% -> 0% of each run, Pallas kernels for 0% -> 0%
where the time goes in v1:
time: 54.1 us; the launch traced here: 53.9 us
  Pallas kernels  44.9 us (83%)
  local copies, waits for them, and re-layouts  8.32 us (15%)
  between operations  0.66 us (1%)
    pallas_call x1, Pallas kernels, body(): pl.pallas_call(functools.partial(kernel, S, H, nb, D, cap), out_shape=(ja...  44.9 us
    unnamed x22, local copies, waits for them, and re-layouts  8.32 us

profile of v1, /device:TPU:0, one launch (start us, length us, event | category | flops | bytes accessed | tf_op | source)
XLA Modules:
  0.0 53.9 jit_solution(16647259830826865921)
XLA Ops:
  0.6 0.0 copy-start.7
  0.6 0.7 %copy-done.7 = s32[64,3]{0,1:T(4,128)S(1)} copy-done((s32[64,3]{0,1:T(4,128)S(1)}, s32[64,3]{0,1:T(4,128)}, u32[]{:S(2)}) %copy-start.7) | copy-done | bytes 792
  1.3 0.0 copy-start.4
  1.3 0.0 copy-start.5
  1.3 0.0 copy-start.6
  1.3 0.1 copy.13.rand_ref
  1.4 0.6 %copy-done.4 = s32[512]{0:T(512)S(1)} copy-done((s32[512]{0:T(512)S(1)}, s32[512]{0:T(512)}, u32[]{:S(2)}) %copy-start.4) | copy-done | bytes 2072
  2.0 0.0 copy-done.5
  2.0 0.0 copy-done.6
  2.0 0.0 copy-start
  2.0 0.9 %copy-done = bf16[512,128]{1,0:T(8,128)(2,1)S(1)} copy-done((bf16[512,128]{1,0:T(8,128)(2,1)S(1)}, bf16[512,128]{1,0:T(8,128)(2,1)}, u32[]{:S(2)}) %copy-start) | copy-done | bytes 131096
  2.9 0.0 copy-start.1
  2.9 0.9 %copy-done.1 = bf16[512,128]{1,0:T(8,128)(2,1)S(1)} copy-done((bf16[512,128]{1,0:T(8,128)(2,1)S(1)}, bf16[512,128]{1,0:T(8,128)(2,1)}, u32[]{:S(2)}) %copy-start.1) | copy-done | bytes 131096
  3.8 0.0 copy-start.2
  3.8 0.9 %copy-done.2 = bf16[512,128]{1,0:T(8,128)(2,1)S(1)} copy-done((bf16[512,128]{1,0:T(8,128)(2,1)S(1)}, bf16[512,128]{1,0:T(8,128)(2,1)}, u32[]{:S(2)}) %copy-start.2) | copy-done | bytes 131096
  4.7 0.0 copy-start.3
  4.7 0.9 %copy-done.3 = bf16[512,128]{1,0:T(8,128)(2,1)S(1)} copy-done((bf16[512,128]{1,0:T(8,128)(2,1)S(1)}, bf16[512,128]{1,0:T(8,128)(2,1)}, u32[]{:S(2)}) %copy-start.3) | copy-done | bytes 131096
  5.6 44.9 %shard_map.119 = (bf16[8,64,128]{2,1,0:T(8,128)(2,1)S(1)}, f32[1,512]{1,0:T(1,128)S(1)}, f32[8,64,128]{2,1,0:T(8,128)S(1)}, f32[8,64,128]{2,1,0:T(8,128)S(1)}, f32[8,64,128]{2,1,0:T(8,128)S(1)}) custom-call(bf16[8,64,128]{2,1,0:T(8,128)(2,1)S(1)} %bitcast.14, bf16[8,64,128]{2,1,0:T(8,128)(2,1)S(1)} %bitcast.15, bf16[8,64,128]{2,1,0:T(8,128)(2,1)S(1)} %bitcast.16, ...), custom_call_target="tpu_custom_call" | custom-call | tf_op jit(solution)/shard_map/pallas_call | solution.py:319
  50.5 0.7 %copy.19 = bf16[512,128]{1,0:T(8,128)(2,1)} copy(bf16[512,128]{1,0:T(8,128)(2,1)S(1)} %bitcast.18) | data formatting | bytes 262144
  51.2 0.6 %copy.20 = f32[512]{0:T(512)} copy(f32[512]{0:T(512)S(1)} %bitcast.20) | data formatting | bytes 4096
  51.8 0.7 %copy.21 = f32[512,128]{1,0:T(8,128)} copy(f32[512,128]{1,0:T(8,128)S(1)} %bitcast.13) | data formatting | bytes 524288
  52.5 0.7 %copy.22 = f32[512,128]{1,0:T(8,128)} copy(f32[512,128]{1,0:T(8,128)S(1)} %bitcast.12) | data formatting | bytes 524288
  53.2 0.7 %copy.23 = f32[512,128]{1,0:T(8,128)} copy(f32[512,128]{1,0:T(8,128)S(1)} %bitcast.11) | data formatting | bytes 524288
Async XLA Ops:
  0.6 0.7 %copy-start.7 = (s32[64,3]{0,1:T(4,128)S(1)}, s32[64,3]{0,1:T(4,128)}, u32[]{:S(2)}) copy-start(s32[64,3]{0,1:T(4,128)} %param.14) | copy-start | bytes 2308
  1.3 0.7 %copy-start.4 = (s32[512]{0:T(512)S(1)}, s32[512]{0:T(512)}, u32[]{:S(2)}) copy-start(s32[512]{0:T(512)} %param.13) | copy-start | bytes 6148
  1.3 0.7 %copy-start.5 = (bf16[128]{0:T(256)(128)(2,1)S(1)}, bf16[128]{0:T(256)(128)(2,1)}, u32[]{:S(2)}) copy-start(bf16[128]{0:T(256)(128)(2,1)} %param.12) | copy-start | bytes 772
  1.3 0.7 %copy-start.6 = (s32[2]{0:T(128)S(1)}, s32[2]{0:T(128)}, u32[]{:S(2)}) copy-start(s32[2]{0:T(128)} %glob_ref.1) | copy-start | bytes 28
  2.0 0.9 %copy-start = (bf16[512,128]{1,0:T(8,128)(2,1)S(1)}, bf16[512,128]{1,0:T(8,128)(2,1)}, u32[]{:S(2)}) copy-start(bf16[512,128]{1,0:T(8,128)(2,1)} %param.8) | copy-start | bytes 393220
  2.9 0.9 %copy-start.1 = (bf16[512,128]{1,0:T(8,128)(2,1)S(1)}, bf16[512,128]{1,0:T(8,128)(2,1)}, u32[]{:S(2)}) copy-start(bf16[512,128]{1,0:T(8,128)(2,1)} %param.9) | copy-start | bytes 393220
  3.8 0.9 %copy-start.2 = (bf16[512,128]{1,0:T(8,128)(2,1)S(1)}, bf16[512,128]{1,0:T(8,128)(2,1)}, u32[]{:S(2)}) copy-start(bf16[512,128]{1,0:T(8,128)(2,1)} %param.10) | copy-start | bytes 393220
  4.7 0.9 %copy-start.3 = (bf16[512,128]{1,0:T(8,128)(2,1)S(1)}, bf16[512,128]{1,0:T(8,128)(2,1)}, u32[]{:S(2)}) copy-start(bf16[512,128]{1,0:T(8,128)(2,1)} %param.11) | copy-start | bytes 393220

commit v2 on v1

v2 whole, which is shorter than its diff:
```python
import functools
import math

import jax
import jax.numpy as jnp
from jax import lax
from jax.experimental import pallas as pl
from jax.experimental.pallas import tpu as pltpu
from jax.sharding import PartitionSpec as P

BLOCK = 64
RAND = 3
GLOBAL = 2
SLOTS = 3 + RAND + GLOBAL
MESH = pl.DeviceIdType.MESH
F32 = jnp.float32
BF16 = jnp.bfloat16
CONTRACT_LAST = (((1,), (1,)), ((), ()))
CONTRACT_FIRST = (((0,), (0,)), ((), ()))
PARTS = 8
VMEM = 63 * 1024 * 1024


def flip(me, bits):
    out = me
    bit = 1
    while bit <= bits:
        if bits & bit:
            out = out + (1 - 2 * lax.rem(lax.div(me, jnp.int32(bit)), jnp.int32(2))) * bit
        bit *= 2
    return out


def kernel(
    S, H, nb, D, cap,
    q_ref, k_ref, v_ref, up_ref, w_ref, lab_ref, rand_ref, glob_ref,
    att_out, loss_out, dq_out, dk_out, dv_out,
    att_ref, loss_ref, dq_ref, dk_ref, dv_ref, lab_s, q_s, up_s, kall, vall, p_s, pb_s, pt_s, ds_s, dst_s, g_s, og, og_in, acc, gsend, grecv, gsum, gall,
    edge_out, edge_in, lmine, lrecv, sidx, roff,
    in_sem, ag_send, ag_recv, l_send, l_recv, o_send, o_recv, e_send, e_recv,
    gp_send, gp_recv, gb_send, gb_recv, out_sem,
):
    me = lax.axis_index("seq")
    hd = lax.axis_index("head")
    N = S * nb
    inv = 1.0 / math.sqrt(D)
    stride = max(1, S // PARTS)
    rows = GLOBAL * BLOCK // PARTS
    T = nb * BLOCK
    half = nb // 2
    WIN = 3 * BLOCK
    mine = pl.ds(me * nb, nb)

    def seq_copy(src, dst, ssem, rsem, peer):
        return pltpu.make_async_remote_copy(
            src_ref=src, dst_ref=dst, send_sem=ssem, recv_sem=rsem,
            device_id={"seq": peer}, device_id_type=MESH)

    local = [
        pltpu.make_async_copy(src, dst, in_sem.at[n])
        for n, (src, dst) in enumerate(
            ((k_ref, kall.at[mine]), (v_ref, vall.at[mine]), (q_ref, q_s), (up_ref, up_s), (lab_ref, lab_s)))
    ]
    for copy in local:
        copy.start()
    results = [
        pltpu.make_async_copy(src, dst, out_sem.at[n])
        for n, (src, dst) in enumerate(
            ((att_ref, att_out), (loss_ref, loss_out), (dq_ref, dq_out), (dk_ref, dk_out), (dv_ref, dv_out)))
    ]

    barrier = pltpu.get_barrier_semaphore()
    for d in range(1, S):
        pl.semaphore_signal(barrier, inc=1, device_id={"seq": flip(me, d)}, device_id_type=MESH)
    for d in range(1, H):
        pl.semaphore_signal(barrier, inc=1, device_id={"head": lax.rem(hd + d, H)}, device_id_type=MESH)
    pl.semaphore_wait(barrier, S - 1 + H - 1)

    full = ((k_ref, kall), (v_ref, vall))
    partner = flip(me, 1)
    sends = []

    def push(a, n, src, owner, lo, count, piece, peer):
        dst = full[a][1].at[pl.ds(owner * nb + lo, count)]
        copy = seq_copy(dst if src is None else src, dst, ag_send.at[a, n], ag_recv.at[a, owner, piece], peer)
        copy.start()
        sends.append(copy)

    def arrived(a, owner, lo, count, piece):
        part = full[a][1].at[pl.ds(owner * nb + lo, count)]
        seq_copy(part, part, ag_send.at[a, 0], ag_recv.at[a, owner, piece], partner).wait_recv()

    two_step = S == 8
    evens = [2, 4] if two_step else list(range(2, S, 2))

    def own(a):
        for d in evens + [1]:
            push(a, d, full[a][0], me, 0, nb, 0, flip(me, d))

    def relay(a):
        for n, d in enumerate(evens):
            owner = flip(me, d)
            arrived(a, owner, 0, nb, 0)
            if two_step:
                push(a, 8 + n, None, owner, n * half, half, n, flip(me, 6 - d))
            push(a, S + 2 + d, None, owner, 0, nb, 0, partner)

    def corner(a):
        if two_step:
            owner = flip(me, 6)
            for n in range(2):
                arrived(a, owner, n * half, half, n)
                push(a, 5 + 2 * n, None, owner, n * half, half, n, partner)

    def finish(a):
        for d in range(1, S, 2):
            owner = flip(me, d)
            if two_step and d == 7:
                for n in range(2):
                    arrived(a, owner, n * half, half, n)
            else:
                arrived(a, owner, 0, nb, 0)

    own(0)
    own(1)

    def tables(s, carry):
        cnt, cnt2 = jnp.int32(0), jnp.int32(0)
        idx = [jnp.int32(3)] * cap
        off = [jnp.int32(-1)] * cap
        for j in range(nb * RAND):
            b = rand_ref[j % RAND, me * nb + j // RAND]
            hit = lax.div(b, jnp.int32(nb)) == s
            c = rand_ref[j % RAND, s * nb + j // RAND]
            hit2 = lax.div(c, jnp.int32(nb)) == me
            place = lax.rem(c, jnp.int32(nb))
            for t in range(cap):
                idx[t] = jnp.where(hit & (cnt == t), j // RAND * SLOTS + 3 + j % RAND, idx[t])
                off[t] = jnp.where(hit2 & (cnt2 == t), place, off[t])
            cnt = cnt + hit.astype(jnp.int32)
            cnt2 = cnt2 + hit2.astype(jnp.int32)
        for t in range(cap):
            sidx[s, t] = idx[t]
            roff[s, t] = off[t]
        return carry

    lax.fori_loop(0, S, tables, 0)
    acc[...] = jnp.zeros_like(acc)

    relay(0)
    relay(1)
    corner(0)
    finish(0)
    for copy in local:
        copy.wait()

    def gather(all_ref, i):
        gi = me * nb + i
        ids = [lax.rem(gi + N - 1, N), gi, lax.rem(gi + 1, N)]
        ids += [rand_ref[r, gi] for r in range(RAND)]
        ids += [glob_ref[r] for r in range(GLOBAL)]
        return jnp.concatenate([all_ref[b] for b in ids], axis=0)

    def by_slot(x):
        return x.T.astype(BF16).reshape(SLOTS, BLOCK, BLOCK)

    def pairs(lo, hi, step):
        def two(t, carry):
            step(2 * t)
            step(2 * t + 1)
            return carry

        lax.fori_loop(lo, hi, two, 0)

    col = lax.broadcasted_iota(jnp.int32, (BLOCK, SLOTS * BLOCK), 1)

    def softmax(i):
        keys = gather(kall, i)
        s = lax.dot_general(q_s[i], keys, CONTRACT_LAST, preferred_element_type=F32) * inv
        gi = me * nb + i
        low = jnp.where(gi == 0, BLOCK, 0)
        void = (col < low) | ((col >= 2 * BLOCK) & (col < jnp.where(gi == N - 1, 3 * BLOCK, 0)))
        s = jnp.where(void, -jnp.inf, s)
        e = jnp.exp(s - jnp.max(s, axis=-1, keepdims=True))
        p = e * (1.0 / jnp.sum(e, axis=-1, keepdims=True))
        p_s[i] = p
        pb_s[i] = p.astype(BF16)
        pt_s[pl.ds(i * SLOTS, SLOTS)] = by_slot(p)

    pairs(0, nb // 4, softmax)
    corner(1)
    pairs(nb // 4, nb // 2, softmax)
    finish(1)

    def attend(i):
        att_ref[i] = jnp.dot(pb_s[i], gather(vall, i), preferred_element_type=F32).astype(BF16)

    pairs(0, nb // 2, attend)

    w = w_ref[...]
    part = lax.dot_general(
        jnp.broadcast_to(w, (16, D)), att_ref[...].reshape(T, D), CONTRACT_LAST,
        preferred_element_type=F32)[0:1]
    lmine[...] = part

    def logit_copy(d, slot):
        return pltpu.make_async_remote_copy(
            src_ref=lmine, dst_ref=lrecv.at[slot], send_sem=l_send.at[d], recv_sem=l_recv.at[slot],
            device_id={"head": lax.rem(hd + d, H)}, device_id_type=MESH)

    for d in range(1, H):
        logit_copy(d, hd).start()
    results[0].start()
    logits = part
    for d in range(1, H):
        slot = lax.rem(hd + d, H)
        logit_copy(d, slot).wait_recv()
        logits = logits + lrecv[slot]
    target = lab_s[...].astype(F32)
    e = jnp.exp(-jnp.abs(logits))
    loss_ref[...] = jnp.maximum(logits, 0.0) + jnp.log1p(e) - target * logits
    results[1].start()
    sig = jnp.where(logits >= 0, 1.0, e) / (1.0 + e)
    dl = jnp.broadcast_to(sig - target, (8, T)).T[:, 0:1]
    grad_out = up_s[...].reshape(T, D).astype(F32) + dl * w.astype(F32)
    g_s[...] = grad_out.astype(BF16).reshape(nb, BLOCK, D)

    terms = ((dst_s, q_s, ds_s), (pt_s, g_s, pb_s))

    def slot_term(a, e):
        return jnp.dot(terms[a][0][e], terms[a][1][lax.div(e, jnp.int32(SLOTS))], preferred_element_type=F32)

    order = sorted(range(1, S), key=lambda d: (-bin(d // 2).count("1"), d % 2, d))

    def out_copy(a, d, peer, slot):
        return seq_copy(og.at[a, peer], og_in.at[a, slot], o_send.at[a, d], o_recv.at[a, slot], peer)

    def send_random(a):
        for d in order:
            peer = flip(me, d)
            for t in range(cap):
                og[a, peer, t] = slot_term(a, sidx[peer, t]).astype(BF16)
            copy = out_copy(a, d, peer, me)
            copy.start()
            sends.append(copy)

    is_part = lax.rem(me, stride) == 0
    my_part = lax.div(me, jnp.int32(stride))

    def part_copy(a, j, owner, slot):
        return seq_copy(
            gsend.at[a, pl.ds(j * rows, rows)], grecv.at[a, slot], gp_send.at[a, j], gp_recv.at[a, slot], owner)

    def share_copy(a, d, peer, slot):
        return seq_copy(gsum.at[a], gall.at[a, slot], gb_send.at[a, d], gb_recv.at[a, slot], peer)

    def send_global(a):
        both = terms[a][2][:, :, (3 + RAND) * BLOCK :].reshape(T, GLOBAL * BLOCK)
        gsend[a] = lax.dot_general(
            both, terms[a][1][...].reshape(T, D), CONTRACT_FIRST, preferred_element_type=F32).astype(BF16)
        for t in range(PARTS):
            j = lax.rem(my_part + t, PARTS)
            owner = j * stride

            @pl.when(owner != me)
            def _():
                part_copy(a, j, owner, me).start()

    def share_global(a):
        @pl.when(is_part)
        def _():
            total = gsend[a, pl.ds(my_part * rows, rows)].astype(F32)
            for d in range(1, S):
                peer = flip(me, d)
                part_copy(a, my_part, peer, peer).wait_recv()
                total = total + grecv[a, peer].astype(F32)
            gsum[a] = total.astype(BF16)
            gall[a, my_part] = gsum[a]
            for d in range(1, S):
                share_copy(a, d, flip(me, d), my_part).start()

    prev, following = lax.rem(me + S - 1, S), lax.rem(me + 1, S)

    def edge_copies(a):
        return (
            seq_copy(edge_out.at[a, 0], edge_in.at[a, 1], e_send.at[a, 0], e_recv.at[a, 1], prev),
            seq_copy(edge_out.at[a, 1], edge_in.at[a, 0], e_send.at[a, 1], e_recv.at[a, 0], following),
        )

    def window(a):
        def step(i):
            left = terms[a][0][pl.ds(i * SLOTS, 3)].reshape(WIN, BLOCK)
            acc[a, pl.ds(i, 3)] += jnp.dot(
                left, terms[a][1][i], preferred_element_type=F32).reshape(3, BLOCK, D)

        pairs(0, nb // 2, step)
        edge_out[a, 0] = acc[a, 0].astype(BF16)
        edge_out[a, 1] = acc[a, nb + 1].astype(BF16)
        for copy in edge_copies(a):
            copy.start()

    def take(a, blocks, places):
        for b in range(nb):
            value = acc[a, 1 + b]
            for block, place in zip(blocks, places):
                value = value + block * (place == b).astype(F32)
            acc[a, 1 + b] = value

    def take_own(a):
        take(a, [slot_term(a, sidx[me, t]) for t in range(cap)], [roff[me, t] for t in range(cap)])

    def take_random(a):
        for d in sorted(order, key=lambda d: (bin(d).count("1"), d)):
            peer = flip(me, d)
            out_copy(a, d, peer, peer).wait_recv()
            take(a, [og_in[a, peer, t].astype(F32) for t in range(cap)], [roff[peer, t] for t in range(cap)])

    def take_rest(a):
        for copy in edge_copies(a):
            copy.wait_recv()
        acc[a, 1] += edge_in[a, 0].astype(F32)
        acc[a, nb] += edge_in[a, 1].astype(F32)
        for t in range(PARTS):
            j = lax.rem(my_part + t, PARTS)

            @pl.when(j * stride != me)
            def _():
                share_copy(a, 0, me, j).wait_recv()

        count = PARTS // GLOBAL
        blocks = [
            gall[a, n * count : (n + 1) * count].astype(F32).reshape(BLOCK, D) for n in range(GLOBAL)]
        take(a, blocks, [glob_ref[n] - me * nb for n in range(GLOBAL)])

    send_global(1)
    send_random(1)

    def score_grad(i):
        dp = lax.dot_general(g_s[i], gather(vall, i), CONTRACT_LAST, preferred_element_type=F32)
        p = p_s[i]
        rd = jnp.sum(p * dp, axis=-1, keepdims=True)
        ds = p * (dp - rd) * inv
        ds_s[i] = ds.astype(BF16)
        dst_s[pl.ds(i * SLOTS, SLOTS)] = by_slot(ds)

    pairs(0, nb // 2, score_grad)
    share_global(1)
    send_global(0)
    send_random(0)
    window(0)
    window(1)
    share_global(0)

    def grad_q(i):
        dq_ref[i] = jnp.dot(ds_s[i], gather(kall, i), preferred_element_type=F32)

    pairs(0, nb // 2, grad_q)
    results[2].start()
    take_own(1)
    take_own(0)
    take_random(1)
    take_rest(1)
    dv_ref[...] = acc[1, 1 : nb + 1]
    results[4].start()
    take_random(0)
    take_rest(0)
    dk_ref[...] = acc[0, 1 : nb + 1]
    results[3].start()

    for copy in results:
        copy.wait()
    for copy in sends:
        copy.wait_send()
    for d in range(1, H):
        logit_copy(d, hd).wait_send()
    for a in range(2):
        for t in range(PARTS):
            j = lax.rem(my_part + t, PARTS)
            owner = j * stride

            @pl.when(owner != me)
            def _():
                part_copy(a, j, owner, me).wait_send()

        for copy in edge_copies(a):
            copy.wait_send()

        @pl.when(is_part)
        def _():
            for d in range(1, S):
                share_copy(a, d, flip(me, d), my_part).wait_send()


def store(*refs):
    count = len(refs) // 2
    copies = [
        pltpu.make_async_copy(refs[n], refs[count + n], refs[-1].at[n]) for n in range(count)]
    for copy in copies:
        copy.start()
    for copy in copies:
        copy.wait()


def body(S, H, queries, key_rows, value_rows, upstream, exit_weight, labels, rand_blocks, glob_blocks):
    T, D = queries.shape
    nb = T // BLOCK
    cap = max(1, (nb * RAND + S - 1) // S)
    rows = GLOBAL * BLOCK // PARTS
    blocked = lambda x: x.reshape(nb, BLOCK, D)
    vmem = pl.BlockSpec(memory_space=pltpu.VMEM)
    smem = pl.BlockSpec(memory_space=pltpu.SMEM)
    hbm = pl.BlockSpec(memory_space=pltpu.HBM)
    dma = pltpu.SemaphoreType.DMA
    results = (
        jax.ShapeDtypeStruct((nb, BLOCK, D), BF16),
        jax.ShapeDtypeStruct((1, T), F32),
        jax.ShapeDtypeStruct((nb, BLOCK, D), F32),
        jax.ShapeDtypeStruct((nb, BLOCK, D), F32),
        jax.ShapeDtypeStruct((nb, BLOCK, D), F32),
    )
    done = pl.pallas_call(
        functools.partial(kernel, S, H, nb, D, cap),
        out_shape=results,
        in_specs=[hbm] * 4 + [vmem, hbm] + [smem] * 2,
        out_specs=[hbm] * 5,
        scratch_shapes=[pltpu.VMEM(x.shape, x.dtype) for x in results] + [
            pltpu.VMEM((1, T), jnp.int32),
            pltpu.VMEM((nb, BLOCK, D), BF16),
            pltpu.VMEM((nb, BLOCK, D), BF16),
            pltpu.VMEM((S * nb, BLOCK, D), BF16),
            pltpu.VMEM((S * nb, BLOCK, D), BF16),
            pltpu.VMEM((nb, BLOCK, SLOTS * BLOCK), F32),
            pltpu.VMEM((nb, BLOCK, SLOTS * BLOCK), BF16),
            pltpu.VMEM((nb * SLOTS, BLOCK, BLOCK), BF16),
            pltpu.VMEM((nb, BLOCK, SLOTS * BLOCK), BF16),
            pltpu.VMEM((nb * SLOTS, BLOCK, BLOCK), BF16),
            pltpu.VMEM((nb, BLOCK, D), BF16),
            pltpu.VMEM((2, S, cap, BLOCK, D), BF16),
            pltpu.VMEM((2, S, cap, BLOCK, D), BF16),
            pltpu.VMEM((2, nb + 2, BLOCK, D), F32),
            pltpu.VMEM((2, GLOBAL * BLOCK, D), BF16),
            pltpu.VMEM((2, S, rows, D), BF16),
            pltpu.VMEM((2, rows, D), BF16),
            pltpu.VMEM((2, PARTS, rows, D), BF16),
            pltpu.VMEM((2, 2, BLOCK, D), BF16),
            pltpu.VMEM((2, 2, BLOCK, D), BF16),
            pltpu.VMEM((1, T), F32),
            pltpu.VMEM((H, 1, T), F32),
            pltpu.SMEM((S, cap), jnp.int32),
            pltpu.SMEM((S, cap), jnp.int32),
            dma((5,)),
            dma((2, 2 * S + 2)), dma((2, S, 2)),
            dma((H,)), dma((H,)),
            dma((2, S)), dma((2, S)),
            dma((2, 2)), dma((2, 2)),
            dma((2, PARTS)), dma((2, S)),
            dma((2, S)), dma((2, PARTS)), dma((5,)),
        ],
        compiler_params=pltpu.CompilerParams(
            collective_id=0, has_side_effects=True, vmem_limit_bytes=VMEM),
    )(
        blocked(queries), blocked(key_rows), blocked(value_rows), blocked(upstream),
        exit_weight.reshape(1, D), labels.reshape(1, T), rand_blocks.T, glob_blocks,
    )
    att, loss, dq, dk, dv = pl.pallas_call(
        store,
        out_shape=results,
        in_specs=[hbm] * 5,
        out_specs=[hbm] * 5,
        scratch_shapes=[dma((5,))],
        compiler_params=pltpu.CompilerParams(vmem_limit_bytes=VMEM),
    )(*done)
    flat = lambda x: x.reshape(T, D)
    return (flat(att), loss.reshape(T), flat(dq), flat(dk), flat(dv))


def solution(mesh):
    placed = (
        P("seq", "head"),
        P("seq", "head"),
        P("seq", "head"),
        P("seq", "head"),
        P("head"),
        P("seq"),
        P(),
        P(),
    )
    return jax.shard_map(
        functools.partial(body, mesh.shape["seq"], mesh.shape["head"]),
        mesh=mesh,
        in_specs=placed,
        out_specs=(
            P("seq", "head"),
            P("seq"),
            P("seq", "head"),
            P("seq", "head"),
            P("seq", "head"),
        ),
        check_vma=False,
    )
```

time: 54.1 us -> 68.6 us (1.27)
  Pallas kernels: 44.9 us -> 67.8 us
  local copies, waits for them, and re-layouts: 8.32 us -> 0 us
    pallas_call x1 -> x2, Pallas kernels: 44.9 us -> 67.8 us  [the longest x1 38.8 us: body(): pl.pallas_call(functools.partial(kernel, S, H, nb, D, cap), out_shape=res...]
    unnamed x22 -> x0, local copies, waits for them, and re-layouts: 8.32 us -> none
where the time goes in v2:
time: 68.6 us; the launch traced here: 68.5 us
  Pallas kernels  67.8 us (99%)
    pallas_call x1, Pallas kernels, body(): pl.pallas_call(functools.partial(kernel, S, H, nb, D, cap), out_shape=res...  38.8 us
    pallas_call x1, Pallas kernels, body(): pl.pallas_call(store, out_shape=results, in_specs=[hbm] * 5, out_specs=[h...  29 us

profile of v2, /device:TPU:0, one launch (start us, length us, event | category | flops | bytes accessed | tf_op | source)
XLA Modules:
  0.0 68.5 jit_solution(8229025633908807577)
XLA Ops:
  0.6 38.8 %shard_map.119 = (bf16[8,64,128]{2,1,0:T(8,128)(2,1)}, f32[1,512]{1,0:T(1,128)}, f32[8,64,128]{2,1,0:T(8,128)}, f32[8,64,128]{2,1,0:T(8,128)}, f32[8,64,128]{2,1,0:T(8,128)}) custom-call(bf16[8,64,128]{2,1,0:T(8,128)(2,1)} %bitcast.12, bf16[8,64,128]{2,1,0:T(8,128)(2,1)} %bitcast.13, bf16[8,64,128]{2,1,0:T(8,128)(2,1)} %bitcast.14, ...), custom_call_target="tpu_custom_call" | custom-call | tf_op jit(solution)/shard_map/pallas_call | solution.py:421
  39.5 29.0 %shard_map.120 = (bf16[8,64,128]{2,1,0:T(8,128)(2,1)}, f32[1,512]{1,0:T(1,128)}, f32[8,64,128]{2,1,0:T(8,128)}, f32[8,64,128]{2,1,0:T(8,128)}, f32[8,64,128]{2,1,0:T(8,128)}) custom-call(bf16[8,64,128]{2,1,0:T(8,128)(2,1)} %get-tuple-element.15.refs_0_, f32[1,512]{1,0:T(1,128)} %get-tuple-element.16.refs_1_, f32[8,64,128]{2,1,0:T(8,128)} %get-tuple-element.17.refs_2_, ...), custom_call_target="tpu_custom_call" | custom-call | tf_op jit(solution)/shard_map/pallas_call | solution.py:465

commit v3 on v2

--- a/solution.py
+++ b/solution.py
@@ -76,18 +76,18 @@
         pl.semaphore_signal(barrier, inc=1, device_id={"head": lax.rem(hd + d, H)}, device_id_type=MESH)
     pl.semaphore_wait(barrier, S - 1 + H - 1)
 
-    full = ((k_ref, kall), (v_ref, vall))
+    full = (kall, vall)
     partner = flip(me, 1)
     sends = []
 
-    def push(a, n, src, owner, lo, count, piece, peer):
-        dst = full[a][1].at[pl.ds(owner * nb + lo, count)]
-        copy = seq_copy(dst if src is None else src, dst, ag_send.at[a, n], ag_recv.at[a, owner, piece], peer)
+    def push(a, n, owner, lo, count, piece, peer):
+        part = full[a].at[pl.ds(owner * nb + lo, count)]
+        copy = seq_copy(part, part, ag_send.at[a, n], ag_recv.at[a, owner, piece], peer)
         copy.start()
         sends.append(copy)
 
     def arrived(a, owner, lo, count, piece):
-        part = full[a][1].at[pl.ds(owner * nb + lo, count)]
+        part = full[a].at[pl.ds(owner * nb + lo, count)]
         seq_copy(part, part, ag_send.at[a, 0], ag_recv.at[a, owner, piece], partner).wait_recv()
 
     two_step = S == 8
@@ -95,22 +95,22 @@
 
     def own(a):
         for d in evens + [1]:
-            push(a, d, full[a][0], me, 0, nb, 0, flip(me, d))
+            push(a, d, me, 0, nb, 0, flip(me, d))
 
     def relay(a):
         for n, d in enumerate(evens):
             owner = flip(me, d)
             arrived(a, owner, 0, nb, 0)
             if two_step:
-                push(a, 8 + n, None, owner, n * half, half, n, flip(me, 6 - d))
-            push(a, S + 2 + d, None, owner, 0, nb, 0, partner)
+                push(a, 8 + n, owner, n * half, half, n, flip(me, 6 - d))
+            push(a, S + 2 + d, owner, 0, nb, 0, partner)
 
     def corner(a):
         if two_step:
             owner = flip(me, 6)
             for n in range(2):
                 arrived(a, owner, n * half, half, n)
-                push(a, 5 + 2 * n, None, owner, n * half, half, n, partner)
+                push(a, 5 + 2 * n, owner, n * half, half, n, partner)
 
     def finish(a):
         for d in range(1, S, 2):
@@ -121,19 +121,19 @@
             else:
                 arrived(a, owner, 0, nb, 0)
 
-    own(0)
-    own(1)
+    for a in range(2):
+        local[a].wait()
+        own(a)
 
     def tables(s, carry):
         cnt, cnt2 = jnp.int32(0), jnp.int32(0)
         idx = [jnp.int32(3)] * cap
         off = [jnp.int32(-1)] * cap
         for j in range(nb * RAND):
-            b = rand_ref[j % RAND, me * nb + j // RAND]
-            hit = lax.div(b, jnp.int32(nb)) == s
-            c = rand_ref[j % RAND, s * nb + j // RAND]
-            hit2 = lax.div(c, jnp.int32(nb)) == me
-            place = lax.rem(c, jnp.int32(nb))
+            b = rand_ref[j % RAND, me * nb + j // RAND] - s * nb
+            hit = (b >= 0) & (b < nb)
+            place = rand_ref[j % RAND, s * nb + j // RAND] - me * nb
+            hit2 = (place >= 0) & (place < nb)
             for t in range(cap):
                 idx[t] = jnp.where(hit & (cnt == t), j // RAND * SLOTS + 3 + j % RAND, idx[t])
                 off[t] = jnp.where(hit2 & (cnt2 == t), place, off[t])
@@ -151,7 +151,7 @@
     relay(1)
     corner(0)
     finish(0)
-    for copy in local:
+    for copy in local[2:]:
         copy.wait()
 
     def gather(all_ref, i):
@@ -392,12 +392,16 @@
 
 
 def store(*refs):
-    count = len(refs) // 2
-    copies = [
-        pltpu.make_async_copy(refs[n], refs[count + n], refs[-1].at[n]) for n in range(count)]
-    for copy in copies:
+    count = (len(refs) - 2) // 3
+    src, dst, buf = (refs[n * count : (n + 1) * count] for n in range(3))
+    loads = [pltpu.make_async_copy(src[n], buf[n], refs[-2].at[n]) for n in range(count)]
+    stores = [pltpu.make_async_copy(buf[n], dst[n], refs[-1].at[n]) for n in range(count)]
+    for copy in loads:
         copy.start()
-    for copy in copies:
+    for load, copy in zip(loads, stores):
+        load.wait()
+        copy.start()
+    for copy in stores:
         copy.wait()
 
 
@@ -467,7 +471,7 @@
         out_shape=results,
         in_specs=[hbm] * 5,
         out_specs=[hbm] * 5,
-        scratch_shapes=[dma((5,))],
+        scratch_shapes=[pltpu.VMEM(x.shape, x.dtype) for x in results] + [dma((5,))] * 2,
         compiler_params=pltpu.CompilerParams(vmem_limit_bytes=VMEM),
     )(*done)
     flat = lambda x: x.reshape(T, D)

time: 68.6 us -> 41.4 us (0.60)
  Pallas kernels: 67.8 us -> 40.6 us
    pallas_call x1, Pallas kernels: 29 us -> 1.99 us  [body(): pl.pallas_call(store, out_shape=results, in_specs=[hbm] * 5, out_specs=[h...]
where the time goes in v3:
time: 41.4 us; the launch traced here: 41.2 us
  Pallas kernels  40.6 us (98%)
  between operations  0.64 us (2%)
    pallas_call x1, Pallas kernels, body(): pl.pallas_call(functools.partial(kernel, S, H, nb, D, cap), out_shape=res...  38.6 us
    pallas_call x1, Pallas kernels, body(): pl.pallas_call(store, out_shape=results, in_specs=[hbm] * 5, out_specs=[h...  1.99 us

profile of v3, /device:TPU:0, one launch (start us, length us, event | category | flops | bytes accessed | tf_op | source)
XLA Modules:
  0.0 41.2 jit_solution(3102913027072825531)
XLA Ops:
  0.6 38.6 %shard_map.119 = (bf16[8,64,128]{2,1,0:T(8,128)(2,1)}, f32[1,512]{1,0:T(1,128)}, f32[8,64,128]{2,1,0:T(8,128)}, f32[8,64,128]{2,1,0:T(8,128)}, f32[8,64,128]{2,1,0:T(8,128)}) custom-call(bf16[8,64,128]{2,1,0:T(8,128)(2,1)} %bitcast.12, bf16[8,64,128]{2,1,0:T(8,128)(2,1)} %bitcast.13, bf16[8,64,128]{2,1,0:T(8,128)(2,1)} %bitcast.14, ...), custom_call_target="tpu_custom_call" | custom-call | tf_op jit(solution)/shard_map/pallas_call | solution.py:425
  39.3 2.0 %shard_map.120 = (bf16[8,64,128]{2,1,0:T(8,128)(2,1)}, f32[1,512]{1,0:T(1,128)}, f32[8,64,128]{2,1,0:T(8,128)}, f32[8,64,128]{2,1,0:T(8,128)}, f32[8,64,128]{2,1,0:T(8,128)}) custom-call(bf16[8,64,128]{2,1,0:T(8,128)(2,1)} %get-tuple-element.15.refs_0_, f32[1,512]{1,0:T(1,128)} %get-tuple-element.16.refs_1_, f32[8,64,128]{2,1,0:T(8,128)} %get-tuple-element.17.refs_2_, ...), custom_call_target="tpu_custom_call" | custom-call | tf_op jit(solution)/shard_map/pallas_call | solution.py:469

commit v4 on v3

--- a/solution.py
+++ b/solution.py
@@ -27,6 +27,17 @@
     while bit <= bits:
         if bits & bit:
             out = out + (1 - 2 * lax.rem(lax.div(me, jnp.int32(bit)), jnp.int32(2))) * bit
+        bit *= 2
+    return out
+
+
+def xor(x, y, n):
+    out = jnp.int32(0)
+    bit = 1
+    while bit < n:
+        a = lax.rem(lax.div(x, jnp.int32(bit)), jnp.int32(2))
+        b = lax.rem(lax.div(y, jnp.int32(bit)), jnp.int32(2))
+        out = out + (a + b - 2 * a * b) * bit
         bit *= 2
     return out
 
@@ -195,54 +206,78 @@
     def attend(i):
         att_ref[i] = jnp.dot(pb_s[i], gather(vall, i), preferred_element_type=F32).astype(BF16)
 
-    pairs(0, nb // 2, attend)
-
     w = w_ref[...]
-    part = lax.dot_general(
-        jnp.broadcast_to(w, (16, D)), att_ref[...].reshape(T, D), CONTRACT_LAST,
-        preferred_element_type=F32)[0:1]
-    lmine[...] = part
-
-    def logit_copy(d, slot):
+    TH = T // 2
+    parts = []
+
+    def logit_copy(h, d, slot):
         return pltpu.make_async_remote_copy(
-            src_ref=lmine, dst_ref=lrecv.at[slot], send_sem=l_send.at[d], recv_sem=l_recv.at[slot],
+            src_ref=lmine.at[h], dst_ref=lrecv.at[h, slot], send_sem=l_send.at[h, d], recv_sem=l_recv.at[h, slot],
             device_id={"head": lax.rem(hd + d, H)}, device_id_type=MESH)
 
-    for d in range(1, H):
-        logit_copy(d, hd).start()
+    for h in range(2):
+        pairs(h * nb // 4, (h + 1) * nb // 4, attend)
+        part = lax.dot_general(
+            jnp.broadcast_to(w, (16, D)), att_ref[h * half : (h + 1) * half].reshape(TH, D), CONTRACT_LAST,
+            preferred_element_type=F32)[0:1]
+        lmine[h] = part
+        parts.append(part)
+        for d in range(1, H):
+            logit_copy(h, d, hd).start()
     results[0].start()
-    logits = part
-    for d in range(1, H):
-        slot = lax.rem(hd + d, H)
-        logit_copy(d, slot).wait_recv()
-        logits = logits + lrecv[slot]
-    target = lab_s[...].astype(F32)
-    e = jnp.exp(-jnp.abs(logits))
-    loss_ref[...] = jnp.maximum(logits, 0.0) + jnp.log1p(e) - target * logits
+
+    def output_grad(h):
+        logits = parts[h]
+        for d in range(1, H):
+            slot = lax.rem(hd + d, H)
+            logit_copy(h, d, slot).wait_recv()
+            logits = logits + lrecv[h, slot]
+        cols = slice(h * TH, (h + 1) * TH)
+        blocks = slice(h * half, (h + 1) * half)
+        target = lab_s[:, cols].astype(F32)
+        e = jnp.exp(-jnp.abs(logits))
+        loss_ref[:, cols] = jnp.maximum(logits, 0.0) + jnp.log1p(e) - target * logits
+        sig = jnp.where(logits >= 0, 1.0, e) / (1.0 + e)
+        dl = jnp.broadcast_to(sig - target, (8, TH)).T[:, 0:1]
+        grad_out = up_s[blocks].reshape(TH, D).astype(F32) + dl * w.astype(F32)
+        g_s[blocks] = grad_out.astype(BF16).reshape(half, BLOCK, D)
+
+    def score_grad(i):
+        dp = lax.dot_general(g_s[i], gather(vall, i), CONTRACT_LAST, preferred_element_type=F32)
+        p = p_s[i]
+        rd = jnp.sum(p * dp, axis=-1, keepdims=True)
+        ds = p * (dp - rd) * inv
+        ds_s[i] = ds.astype(BF16)
+        dst_s[pl.ds(i * SLOTS, SLOTS)] = by_slot(ds)
+
+    output_grad(0)
+    pairs(0, nb // 4, score_grad)
+    output_grad(1)
     results[1].start()
-    sig = jnp.where(logits >= 0, 1.0, e) / (1.0 + e)
-    dl = jnp.broadcast_to(sig - target, (8, T)).T[:, 0:1]
-    grad_out = up_s[...].reshape(T, D).astype(F32) + dl * w.astype(F32)
-    g_s[...] = grad_out.astype(BF16).reshape(nb, BLOCK, D)
 
     terms = ((dst_s, q_s, ds_s), (pt_s, g_s, pb_s))
 
     def slot_term(a, e):
         return jnp.dot(terms[a][0][e], terms[a][1][lax.div(e, jnp.int32(SLOTS))], preferred_element_type=F32)
 
-    order = sorted(range(1, S), key=lambda d: (-bin(d // 2).count("1"), d % 2, d))
-
     def out_copy(a, d, peer, slot):
         return seq_copy(og.at[a, peer], og_in.at[a, slot], o_send.at[a, d], o_recv.at[a, slot], peer)
 
+    def peers(step):
+        def one(n, carry):
+            d = S - 1 - n
+            step(d, xor(me, d, S))
+            return carry
+
+        lax.fori_loop(0, S - 1, one, 0)
+
     def send_random(a):
-        for d in order:
-            peer = flip(me, d)
+        def step(d, peer):
             for t in range(cap):
                 og[a, peer, t] = slot_term(a, sidx[peer, t]).astype(BF16)
-            copy = out_copy(a, d, peer, me)
-            copy.start()
-            sends.append(copy)
+            out_copy(a, d, peer, me).start()
+
+        peers(step)
 
     is_part = lax.rem(me, stride) == 0
     my_part = lax.div(me, jnp.int32(stride))
@@ -253,18 +288,24 @@
 
     def share_copy(a, d, peer, slot):
         return seq_copy(gsum.at[a], gall.at[a, slot], gb_send.at[a, d], gb_recv.at[a, slot], peer)
+
+    def parts_loop(step):
+        def one(t, carry):
+            j = lax.rem(my_part + t, PARTS)
+
+            @pl.when(j * stride != me)
+            def _():
+                step(j)
+
+            return carry
+
+        lax.fori_loop(0, PARTS, one, 0)
 
     def send_global(a):
         both = terms[a][2][:, :, (3 + RAND) * BLOCK :].reshape(T, GLOBAL * BLOCK)
         gsend[a] = lax.dot_general(
             both, terms[a][1][...].reshape(T, D), CONTRACT_FIRST, preferred_element_type=F32).astype(BF16)
-        for t in range(PARTS):
-            j = lax.rem(my_part + t, PARTS)
-            owner = j * stride
-
-            @pl.when(owner != me)
-            def _():
-                part_copy(a, j, owner, me).start()
+        parts_loop(lambda j: part_copy(a, j, j * stride, me).start())
 
     def share_global(a):
         @pl.when(is_part)
@@ -276,8 +317,7 @@
                 total = total + grecv[a, peer].astype(F32)
             gsum[a] = total.astype(BF16)
             gall[a, my_part] = gsum[a]
-            for d in range(1, S):
-                share_copy(a, d, flip(me, d), my_part).start()
+            peers(lambda d, peer: share_copy(a, d, peer, my_part).start())
 
     prev, following = lax.rem(me + S - 1, S), lax.rem(me + 1, S)
 
@@ -310,23 +350,18 @@
         take(a, [slot_term(a, sidx[me, t]) for t in range(cap)], [roff[me, t] for t in range(cap)])
 
     def take_random(a):
-        for d in sorted(order, key=lambda d: (bin(d).count("1"), d)):
-            peer = flip(me, d)
+        def step(d, peer):
             out_copy(a, d, peer, peer).wait_recv()
             take(a, [og_in[a, peer, t].astype(F32) for t in range(cap)], [roff[peer, t] for t in range(cap)])
+
+        peers(step)
 
     def take_rest(a):
         for copy in edge_copies(a):
             copy.wait_recv()
         acc[a, 1] += edge_in[a, 0].astype(F32)
         acc[a, nb] += edge_in[a, 1].astype(F32)
-        for t in range(PARTS):
-            j = lax.rem(my_part + t, PARTS)
-
-            @pl.when(j * stride != me)
-            def _():
-                share_copy(a, 0, me, j).wait_recv()
-
+        parts_loop(lambda j: share_copy(a, 0, me, j).wait_recv())
         count = PARTS // GLOBAL
         blocks = [
             gall[a, n * count : (n + 1) * count].astype(F32).reshape(BLOCK, D) for n in range(GLOBAL)]
@@ -335,15 +370,7 @@
     send_global(1)
     send_random(1)
 
-    def score_grad(i):
-        dp = lax.dot_general(g_s[i], gather(vall, i), CONTRACT_LAST, preferred_element_type=F32)
-        p = p_s[i]
-        rd = jnp.sum(p * dp, axis=-1, keepdims=True)
-        ds = p * (dp - rd) * inv
-        ds_s[i] = ds.astype(BF16)
-        dst_s[pl.ds(i * SLOTS, SLOTS)] = by_slot(ds)
-
-    pairs(0, nb // 2, score_grad)
+    pairs(nb // 4, nb // 2, score_grad)
     share_global(1)
     send_global(0)
     send_random(0)
@@ -371,24 +398,18 @@
         copy.wait()
     for copy in sends:
         copy.wait_send()
-    for d in range(1, H):
-        logit_copy(d, hd).wait_send()
+    for h in range(2):
+        for d in range(1, H):
+            logit_copy(h, d, hd).wait_send()
     for a in range(2):
-        for t in range(PARTS):
-            j = lax.rem(my_part + t, PARTS)
-            owner = j * stride
-
-            @pl.when(owner != me)
-            def _():
-                part_copy(a, j, owner, me).wait_send()
-
+        peers(lambda d, peer: out_copy(a, d, peer, me).wait_send())
+        parts_loop(lambda j: part_copy(a, j, j * stride, me).wait_send())
         for copy in edge_copies(a):
             copy.wait_send()
 
         @pl.when(is_part)
         def _():
-            for d in range(1, S):
-                share_copy(a, d, flip(me, d), my_part).wait_send()
+            peers(lambda d, peer: share_copy(a, d, peer, my_part).wait_send())
 
 
 def store(*refs):
@@ -448,13 +469,13 @@
             pltpu.VMEM((2, PARTS, rows, D), BF16),
             pltpu.VMEM((2, 2, BLOCK, D), BF16),
             pltpu.VMEM((2, 2, BLOCK, D), BF16),
-            pltpu.VMEM((1, T), F32),
-            pltpu.VMEM((H, 1, T), F32),
+            pltpu.VMEM((2, 1, T // 2), F32),
+            pltpu.VMEM((2, H, 1, T // 2), F32),
             pltpu.SMEM((S, cap), jnp.int32),
             pltpu.SMEM((S, cap), jnp.int32),
             dma((5,)),
             dma((2, 2 * S + 2)), dma((2, S, 2)),
-            dma((H,)), dma((H,)),
+            dma((2, H)), dma((2, H)),
             dma((2, S)), dma((2, S)),
             dma((2, 2)), dma((2, 2)),
             dma((2, PARTS)), dma((2, S)),

time: 41.4 us -> 42.5 us (1.027)
  Pallas kernels: 40.6 us -> 41.7 us
    pallas_call x1, Pallas kernels: 38.6 us -> 39.7 us  [body(): pl.pallas_call(functools.partial(kernel, S, H, nb, D, cap), out_shape=res...]
where the time goes in v4:
time: 42.5 us; the launch traced here: 42.3 us
  Pallas kernels  41.7 us (98%)
  between operations  0.64 us (2%)
    pallas_call x1, Pallas kernels, body(): pl.pallas_call(functools.partial(kernel, S, H, nb, D, cap), out_shape=res...  39.7 us
    pallas_call x1, Pallas kernels, body(): pl.pallas_call(store, out_shape=results, in_specs=[hbm] * 5, out_specs=[h...  1.99 us

profile of v4, /device:TPU:0, one launch (start us, length us, event | category | flops | bytes accessed | tf_op | source)
XLA Modules:
  0.0 42.3 jit_solution(7827619353064893298)
XLA Ops:
  0.6 39.7 %shard_map.119 = (bf16[8,64,128]{2,1,0:T(8,128)(2,1)}, f32[1,512]{1,0:T(1,128)}, f32[8,64,128]{2,1,0:T(8,128)}, f32[8,64,128]{2,1,0:T(8,128)}, f32[8,64,128]{2,1,0:T(8,128)}) custom-call(bf16[8,64,128]{2,1,0:T(8,128)(2,1)} %bitcast.12, bf16[8,64,128]{2,1,0:T(8,128)(2,1)} %bitcast.13, bf16[8,64,128]{2,1,0:T(8,128)(2,1)} %bitcast.14, ...), custom_call_target="tpu_custom_call" | custom-call | tf_op jit(solution)/shard_map/pallas_call | solution.py:446
  40.3 2.0 %shard_map.120 = (bf16[8,64,128]{2,1,0:T(8,128)(2,1)}, f32[1,512]{1,0:T(1,128)}, f32[8,64,128]{2,1,0:T(8,128)}, f32[8,64,128]{2,1,0:T(8,128)}, f32[8,64,128]{2,1,0:T(8,128)}) custom-call(bf16[8,64,128]{2,1,0:T(8,128)(2,1)} %get-tuple-element.15.refs_0_, f32[1,512]{1,0:T(1,128)} %get-tuple-element.16.refs_1_, f32[8,64,128]{2,1,0:T(8,128)} %get-tuple-element.17.refs_2_, ...), custom_call_target="tpu_custom_call" | custom-call | tf_op jit(solution)/shard_map/pallas_call | solution.py:490

commit v5 on v4

--- a/solution.py
+++ b/solution.py
@@ -27,17 +27,6 @@
     while bit <= bits:
         if bits & bit:
             out = out + (1 - 2 * lax.rem(lax.div(me, jnp.int32(bit)), jnp.int32(2))) * bit
-        bit *= 2
-    return out
-
-
-def xor(x, y, n):
-    out = jnp.int32(0)
-    bit = 1
-    while bit < n:
-        a = lax.rem(lax.div(x, jnp.int32(bit)), jnp.int32(2))
-        b = lax.rem(lax.div(y, jnp.int32(bit)), jnp.int32(2))
-        out = out + (a + b - 2 * a * b) * bit
         bit *= 2
     return out
 
@@ -61,6 +50,7 @@
     half = nb // 2
     WIN = 3 * BLOCK
     mine = pl.ds(me * nb, nb)
+    at = [flip(me, d) for d in range(S)]
 
     def seq_copy(src, dst, ssem, rsem, peer):
         return pltpu.make_async_remote_copy(
@@ -82,13 +72,13 @@
 
     barrier = pltpu.get_barrier_semaphore()
     for d in range(1, S):
-        pl.semaphore_signal(barrier, inc=1, device_id={"seq": flip(me, d)}, device_id_type=MESH)
+        pl.semaphore_signal(barrier, inc=1, device_id={"seq": at[d]}, device_id_type=MESH)
     for d in range(1, H):
         pl.semaphore_signal(barrier, inc=1, device_id={"head": lax.rem(hd + d, H)}, device_id_type=MESH)
     pl.semaphore_wait(barrier, S - 1 + H - 1)
 
     full = (kall, vall)
-    partner = flip(me, 1)
+    partner = at[1]
     sends = []
 
     def push(a, n, owner, lo, count, piece, peer):
@@ -106,26 +96,26 @@
 
     def own(a):
         for d in evens + [1]:
-            push(a, d, me, 0, nb, 0, flip(me, d))
+            push(a, d, me, 0, nb, 0, at[d])
 
     def relay(a):
         for n, d in enumerate(evens):
-            owner = flip(me, d)
+            owner = at[d]
             arrived(a, owner, 0, nb, 0)
             if two_step:
-                push(a, 8 + n, owner, n * half, half, n, flip(me, 6 - d))
+                push(a, 8 + n, owner, n * half, half, n, at[6 - d])
             push(a, S + 2 + d, owner, 0, nb, 0, partner)
 
     def corner(a):
         if two_step:
-            owner = flip(me, 6)
+            owner = at[6]
             for n in range(2):
                 arrived(a, owner, n * half, half, n)
                 push(a, 5 + 2 * n, owner, n * half, half, n, partner)
 
     def finish(a):
         for d in range(1, S, 2):
-            owner = flip(me, d)
+            owner = at[d]
             if two_step and d == 7:
                 for n in range(2):
                     arrived(a, owner, n * half, half, n)
@@ -176,12 +166,8 @@
         return x.T.astype(BF16).reshape(SLOTS, BLOCK, BLOCK)
 
     def pairs(lo, hi, step):
-        def two(t, carry):
-            step(2 * t)
-            step(2 * t + 1)
-            return carry
-
-        lax.fori_loop(lo, hi, two, 0)
+        for i in range(2 * lo, 2 * hi):
+            step(i)
 
     col = lax.broadcasted_iota(jnp.int32, (BLOCK, SLOTS * BLOCK), 1)
 
@@ -264,12 +250,8 @@
         return seq_copy(og.at[a, peer], og_in.at[a, slot], o_send.at[a, d], o_recv.at[a, slot], peer)
 
     def peers(step):
-        def one(n, carry):
-            d = S - 1 - n
-            step(d, xor(me, d, S))
-            return carry
-
-        lax.fori_loop(0, S - 1, one, 0)
+        for d in range(S - 1, 0, -1):
+            step(d, at[d])
 
     def send_random(a):
         def step(d, peer):
@@ -279,7 +261,7 @@
 
         peers(step)
 
-    is_part = lax.rem(me, stride) == 0
+    on_part = (lambda f: f()) if stride == 1 else pl.when(lax.rem(me, stride) == 0)
     my_part = lax.div(me, jnp.int32(stride))
 
     def part_copy(a, j, owner, slot):
@@ -290,16 +272,12 @@
         return seq_copy(gsum.at[a], gall.at[a, slot], gb_send.at[a, d], gb_recv.at[a, slot], peer)
 
     def parts_loop(step):
-        def one(t, carry):
+        for t in range(1 if stride == 1 else 0, PARTS):
             j = lax.rem(my_part + t, PARTS)
-
-            @pl.when(j * stride != me)
-            def _():
+            if stride == 1:
                 step(j)
-
-            return carry
-
-        lax.fori_loop(0, PARTS, one, 0)
+            else:
+                pl.when(j * stride != me)(functools.partial(step, j))
 
     def send_global(a):
         both = terms[a][2][:, :, (3 + RAND) * BLOCK :].reshape(T, GLOBAL * BLOCK)
@@ -308,11 +286,11 @@
         parts_loop(lambda j: part_copy(a, j, j * stride, me).start())
 
     def share_global(a):
-        @pl.when(is_part)
+        @on_part
         def _():
             total = gsend[a, pl.ds(my_part * rows, rows)].astype(F32)
             for d in range(1, S):
-                peer = flip(me, d)
+                peer = at[d]
                 part_copy(a, my_part, peer, peer).wait_recv()
                 total = total + grecv[a, peer].astype(F32)
             gsum[a] = total.astype(BF16)
@@ -394,8 +372,6 @@
     dk_ref[...] = acc[0, 1 : nb + 1]
     results[3].start()
 
-    for copy in results:
-        copy.wait()
     for copy in sends:
         copy.wait_send()
     for h in range(2):
@@ -407,9 +383,11 @@
         for copy in edge_copies(a):
             copy.wait_send()
 
-        @pl.when(is_part)
+        @on_part
         def _():
             peers(lambda d, peer: share_copy(a, d, peer, my_part).wait_send())
+    for copy in results:
+        copy.wait()
 
 
 def store(*refs):

time: 42.5 us -> 41.4 us (0.974)
  Pallas kernels: 41.7 us -> 40.6 us
    pallas_call x1, Pallas kernels: 39.7 us -> 38.6 us  [body(): pl.pallas_call(functools.partial(kernel, S, H, nb, D, cap), out_shape=res...]
where the time goes in v5:
time: 41.4 us; the launch traced here: 41.3 us
  Pallas kernels  40.6 us (98%)
  between operations  0.64 us (2%)
    pallas_call x1, Pallas kernels, body(): pl.pallas_call(functools.partial(kernel, S, H, nb, D, cap), out_shape=res...  38.6 us
    pallas_call x1, Pallas kernels, body(): pl.pallas_call(store, out_shape=results, in_specs=[hbm] * 5, out_specs=[h...  1.99 us

profile of v5, /device:TPU:0, one launch (start us, length us, event | category | flops | bytes accessed | tf_op | source)
XLA Modules:
  0.0 41.3 jit_solution(17858701107765698303)
XLA Ops:
  0.6 38.6 %shard_map.119 = (bf16[8,64,128]{2,1,0:T(8,128)(2,1)}, f32[1,512]{1,0:T(1,128)}, f32[8,64,128]{2,1,0:T(8,128)}, f32[8,64,128]{2,1,0:T(8,128)}, f32[8,64,128]{2,1,0:T(8,128)}) custom-call(bf16[8,64,128]{2,1,0:T(8,128)(2,1)} %bitcast.12, bf16[8,64,128]{2,1,0:T(8,128)(2,1)} %bitcast.13, bf16[8,64,128]{2,1,0:T(8,128)(2,1)} %bitcast.14, ...), custom_call_target="tpu_custom_call" | custom-call | tf_op jit(solution)/shard_map/pallas_call | solution.py:424
  39.3 2.0 %shard_map.120 = (bf16[8,64,128]{2,1,0:T(8,128)(2,1)}, f32[1,512]{1,0:T(1,128)}, f32[8,64,128]{2,1,0:T(8,128)}, f32[8,64,128]{2,1,0:T(8,128)}, f32[8,64,128]{2,1,0:T(8,128)}) custom-call(bf16[8,64,128]{2,1,0:T(8,128)(2,1)} %get-tuple-element.15.refs_0_, f32[1,512]{1,0:T(1,128)} %get-tuple-element.16.refs_1_, f32[8,64,128]{2,1,0:T(8,128)} %get-tuple-element.17.refs_2_, ...), custom_call_target="tpu_custom_call" | custom-call | tf_op jit(solution)/shard_map/pallas_call | solution.py:468

commit v6 on v5

--- a/solution.py
+++ b/solution.py
@@ -237,7 +237,6 @@
         dst_s[pl.ds(i * SLOTS, SLOTS)] = by_slot(ds)
 
     output_grad(0)
-    pairs(0, nb // 4, score_grad)
     output_grad(1)
     results[1].start()
 
@@ -249,8 +248,10 @@
     def out_copy(a, d, peer, slot):
         return seq_copy(og.at[a, peer], og_in.at[a, slot], o_send.at[a, d], o_recv.at[a, slot], peer)
 
+    order = [6, 4, 2, 7, 5, 3, 1] if two_step else list(range(S - 1, 0, -1))
+
     def peers(step):
-        for d in range(S - 1, 0, -1):
+        for d in order:
             step(d, at[d])
 
     def send_random(a):
@@ -264,12 +265,11 @@
     on_part = (lambda f: f()) if stride == 1 else pl.when(lax.rem(me, stride) == 0)
     my_part = lax.div(me, jnp.int32(stride))
 
-    def part_copy(a, j, owner, slot):
-        return seq_copy(
-            gsend.at[a, pl.ds(j * rows, rows)], grecv.at[a, slot], gp_send.at[a, j], gp_recv.at[a, slot], owner)
-
-    def share_copy(a, d, peer, slot):
-        return seq_copy(gsum.at[a], gall.at[a, slot], gb_send.at[a, d], gb_recv.at[a, slot], peer)
+    def part_copy(j, owner, slot):
+        return seq_copy(gsend.at[j], grecv.at[slot], gp_send.at[j], gp_recv.at[slot], owner)
+
+    def share_copy(d, peer, slot):
+        return seq_copy(gsum, gall.at[slot], gb_send.at[d], gb_recv.at[slot], peer)
 
     def parts_loop(step):
         for t in range(1 if stride == 1 else 0, PARTS):
@@ -279,23 +279,24 @@
             else:
                 pl.when(j * stride != me)(functools.partial(step, j))
 
-    def send_global(a):
-        both = terms[a][2][:, :, (3 + RAND) * BLOCK :].reshape(T, GLOBAL * BLOCK)
-        gsend[a] = lax.dot_general(
-            both, terms[a][1][...].reshape(T, D), CONTRACT_FIRST, preferred_element_type=F32).astype(BF16)
-        parts_loop(lambda j: part_copy(a, j, j * stride, me).start())
-
-    def share_global(a):
+    def send_global():
+        for a in range(2):
+            both = terms[a][2][:, :, (3 + RAND) * BLOCK :].reshape(T, GLOBAL * BLOCK)
+            gsend[:, a] = lax.dot_general(
+                both, terms[a][1][...].reshape(T, D), CONTRACT_FIRST, preferred_element_type=F32
+            ).astype(BF16).reshape(PARTS, rows, D)
+        parts_loop(lambda j: part_copy(j, j * stride, me).start())
+
+    def share_global():
         @on_part
         def _():
-            total = gsend[a, pl.ds(my_part * rows, rows)].astype(F32)
+            total = gsend[my_part].astype(F32)
             for d in range(1, S):
-                peer = at[d]
-                part_copy(a, my_part, peer, peer).wait_recv()
-                total = total + grecv[a, peer].astype(F32)
-            gsum[a] = total.astype(BF16)
-            gall[a, my_part] = gsum[a]
-            peers(lambda d, peer: share_copy(a, d, peer, my_part).start())
+                part_copy(my_part, at[d], at[d]).wait_recv()
+                total = total + grecv[at[d]].astype(F32)
+            gsum[...] = total.astype(BF16)
+            gall[my_part] = gsum[...]
+            peers(lambda d, peer: share_copy(d, peer, my_part).start())
 
     prev, following = lax.rem(me + S - 1, S), lax.rem(me + 1, S)
 
@@ -339,22 +340,18 @@
             copy.wait_recv()
         acc[a, 1] += edge_in[a, 0].astype(F32)
         acc[a, nb] += edge_in[a, 1].astype(F32)
-        parts_loop(lambda j: share_copy(a, 0, me, j).wait_recv())
         count = PARTS // GLOBAL
         blocks = [
-            gall[a, n * count : (n + 1) * count].astype(F32).reshape(BLOCK, D) for n in range(GLOBAL)]
+            gall[n * count : (n + 1) * count, a].astype(F32).reshape(BLOCK, D) for n in range(GLOBAL)]
         take(a, blocks, [glob_ref[n] - me * nb for n in range(GLOBAL)])
 
-    send_global(1)
     send_random(1)
-
-    pairs(nb // 4, nb // 2, score_grad)
-    share_global(1)
-    send_global(0)
+    pairs(0, nb // 2, score_grad)
+    send_global()
     send_random(0)
     window(0)
     window(1)
-    share_global(0)
+    share_global()
 
     def grad_q(i):
         dq_ref[i] = jnp.dot(ds_s[i], gather(kall, i), preferred_element_type=F32)
@@ -364,6 +361,7 @@
     take_own(1)
     take_own(0)
     take_random(1)
+    parts_loop(lambda j: share_copy(0, me, j).wait_recv())
     take_rest(1)
     dv_ref[...] = acc[1, 1 : nb + 1]
     results[4].start()
@@ -379,13 +377,15 @@
             logit_copy(h, d, hd).wait_send()
     for a in range(2):
         peers(lambda d, peer: out_copy(a, d, peer, me).wait_send())
-        parts_loop(lambda j: part_copy(a, j, j * stride, me).wait_send())
         for copy in edge_copies(a):
             copy.wait_send()
 
-        @on_part
-        def _():
-            peers(lambda d, peer: share_copy(a, d, peer, my_part).wait_send())
+    parts_loop(lambda j: part_copy(j, j * stride, me).wait_send())
+
+    @on_part
+    def _():
+        peers(lambda d, peer: share_copy(d, peer, my_part).wait_send())
+
     for copy in results:
         copy.wait()
 
@@ -441,10 +441,10 @@
             pltpu.VMEM((2, S, cap, BLOCK, D), BF16),
             pltpu.VMEM((2, S, cap, BLOCK, D), BF16),
             pltpu.VMEM((2, nb + 2, BLOCK, D), F32),
-            pltpu.VMEM((2, GLOBAL * BLOCK, D), BF16),
-            pltpu.VMEM((2, S, rows, D), BF16),
+            pltpu.VMEM((PARTS, 2, rows, D), BF16),
+            pltpu.VMEM((S, 2, rows, D), BF16),
             pltpu.VMEM((2, rows, D), BF16),
-            pltpu.VMEM((2, PARTS, rows, D), BF16),
+            pltpu.VMEM((PARTS, 2, rows, D), BF16),
             pltpu.VMEM((2, 2, BLOCK, D), BF16),
             pltpu.VMEM((2, 2, BLOCK, D), BF16),
             pltpu.VMEM((2, 1, T // 2), F32),
@@ -456,8 +456,8 @@
             dma((2, H)), dma((2, H)),
             dma((2, S)), dma((2, S)),
             dma((2, 2)), dma((2, 2)),
-            dma((2, PARTS)), dma((2, S)),
-            dma((2, S)), dma((2, PARTS)), dma((5,)),
+            dma((PARTS,)), dma((S,)),
+            dma((S,)), dma((PARTS,)), dma((5,)),
         ],
         compiler_params=pltpu.CompilerParams(
             collective_id=0, has_side_effects=True, vmem_limit_bytes=VMEM),

time: 41.4 us -> 41 us (level)
  no operation moved by 1% of the time
where the time goes in v6:
time: 41 us; the launch traced here: 40.9 us
  Pallas kernels  40.2 us (98%)
  between operations  0.64 us (2%)
    pallas_call x1, Pallas kernels, body(): pl.pallas_call(functools.partial(kernel, S, H, nb, D, cap), out_shape=res...  38.2 us
    pallas_call x1, Pallas kernels, body(): pl.pallas_call(store, out_shape=results, in_specs=[hbm] * 5, out_specs=[h...  1.99 us

profile of v6, /device:TPU:0, one launch (start us, length us, event | category | flops | bytes accessed | tf_op | source)
XLA Modules:
  0.0 40.9 jit_solution(18289999540127609128)
XLA Ops:
  0.6 38.2 %shard_map.119 = (bf16[8,64,128]{2,1,0:T(8,128)(2,1)}, f32[1,512]{1,0:T(1,128)}, f32[8,64,128]{2,1,0:T(8,128)}, f32[8,64,128]{2,1,0:T(8,128)}, f32[8,64,128]{2,1,0:T(8,128)}) custom-call(bf16[8,64,128]{2,1,0:T(8,128)(2,1)} %bitcast.12, bf16[8,64,128]{2,1,0:T(8,128)(2,1)} %bitcast.13, bf16[8,64,128]{2,1,0:T(8,128)(2,1)} %bitcast.14, ...), custom_call_target="tpu_custom_call" | custom-call | tf_op jit(solution)/shard_map/pallas_call | solution.py:424
  38.9 2.0 %shard_map.120 = (bf16[8,64,128]{2,1,0:T(8,128)(2,1)}, f32[1,512]{1,0:T(1,128)}, f32[8,64,128]{2,1,0:T(8,128)}, f32[8,64,128]{2,1,0:T(8,128)}, f32[8,64,128]{2,1,0:T(8,128)}) custom-call(bf16[8,64,128]{2,1,0:T(8,128)(2,1)} %get-tuple-element.15.refs_0_, f32[1,512]{1,0:T(1,128)} %get-tuple-element.16.refs_1_, f32[8,64,128]{2,1,0:T(8,128)} %get-tuple-element.17.refs_2_, ...), custom_call_target="tpu_custom_call" | custom-call | tf_op jit(solution)/shard_map/pallas_call | solution.py:468

commit v7 on v6

--- a/solution.py
+++ b/solution.py
@@ -38,7 +38,7 @@
     att_ref, loss_ref, dq_ref, dk_ref, dv_ref, lab_s, q_s, up_s, kall, vall, p_s, pb_s, pt_s, ds_s, dst_s, g_s, og, og_in, acc, gsend, grecv, gsum, gall,
     edge_out, edge_in, lmine, lrecv, sidx, roff,
     in_sem, ag_send, ag_recv, l_send, l_recv, o_send, o_recv, e_send, e_recv,
-    gp_send, gp_recv, gb_send, gb_recv, out_sem,
+    gp_send, gp_recv, gb_send, gb_recv, out_sem, dlr_s, cs, cs_in, c_send, c_recv,
 ):
     me = lax.axis_index("seq")
     hd = lax.axis_index("head")
@@ -187,6 +187,59 @@
     pairs(0, nb // 4, softmax)
     corner(1)
     pairs(nb // 4, nb // 2, softmax)
+    terms = ((dst_s, q_s, ds_s), (pt_s, g_s, pb_s))
+
+    def slot_term(a, e, right=None):
+        right = terms[a][1] if right is None else right
+        return jnp.dot(terms[a][0][e], right[lax.div(e, jnp.int32(SLOTS))], preferred_element_type=F32)
+
+    def out_copy(a, d, peer, slot):
+        return seq_copy(og.at[a, peer], og_in.at[a, slot], o_send.at[a, d], o_recv.at[a, slot], peer)
+
+    order = [6, 4, 2, 7, 5, 3, 1] if two_step else list(range(S - 1, 0, -1))
+
+    def peers(step):
+        for d in order:
+            step(d, at[d])
+
+    def send_random(a, right=None):
+        def step(d, peer):
+            for t in range(cap):
+                og[a, peer, t] = slot_term(a, sidx[peer, t], right).astype(BF16)
+            out_copy(a, d, peer, me).start()
+
+        peers(step)
+
+    row = lax.broadcasted_iota(jnp.int32, (16, BLOCK), 0)
+
+    def corr_copy(d, peer, slot):
+        return seq_copy(cs.at[peer], cs_in.at[slot], c_send.at[d], c_recv.at[slot], peer)
+
+    def two_rows(x, t, row=row):
+        high = x.astype(BF16).astype(F32)
+        return jnp.where(row == 2 * t, high, jnp.where(row == 2 * t + 1, x - high, 0.0))
+
+    def send_corrections():
+        def step(d, peer):
+            rows16 = jnp.zeros((16, BLOCK), F32)
+            for t in range(cap):
+                e = sidx[peer, t]
+                r = lax.dot_general(
+                    dlr_s[lax.div(e, jnp.int32(SLOTS))], pt_s[e], CONTRACT_LAST, preferred_element_type=F32)
+                rows16 = rows16 + two_rows(r[0:1] + r[1:2], t)
+            cs[peer] = jnp.concatenate([rows16, jnp.zeros_like(rows16)], axis=1).astype(BF16)
+            corr_copy(d, peer, me).start()
+
+        peers(step)
+
+    def correction(peer, t):
+        x = cs_in[peer][:, :BLOCK].astype(F32)
+        x = jnp.where((row >= 2 * t) & (row < 2 * t + 2), x, 0.0).astype(BF16)
+        return lax.dot_general(
+            x, jnp.broadcast_to(w_ref[...], (16, D)), CONTRACT_FIRST, preferred_element_type=F32)
+
+    send_random(1, up_s)
+
     finish(1)
 
     def attend(i):
@@ -226,6 +279,9 @@
         sig = jnp.where(logits >= 0, 1.0, e) / (1.0 + e)
         dl = jnp.broadcast_to(sig - target, (8, TH)).T[:, 0:1]
         grad_out = up_s[blocks].reshape(TH, D).astype(F32) + dl * w.astype(F32)
+        rows16 = two_rows(sig - target, 0, lax.broadcasted_iota(jnp.int32, (16, TH), 0)).astype(BF16)
+        for b in range(half):
+            dlr_s[h * half + b] = rows16[:, b * BLOCK : (b + 1) * BLOCK]
         g_s[blocks] = grad_out.astype(BF16).reshape(half, BLOCK, D)
 
     def score_grad(i):
@@ -239,28 +295,6 @@
     output_grad(0)
     output_grad(1)
     results[1].start()
-
-    terms = ((dst_s, q_s, ds_s), (pt_s, g_s, pb_s))
-
-    def slot_term(a, e):
-        return jnp.dot(terms[a][0][e], terms[a][1][lax.div(e, jnp.int32(SLOTS))], preferred_element_type=F32)
-
-    def out_copy(a, d, peer, slot):
-        return seq_copy(og.at[a, peer], og_in.at[a, slot], o_send.at[a, d], o_recv.at[a, slot], peer)
-
-    order = [6, 4, 2, 7, 5, 3, 1] if two_step else list(range(S - 1, 0, -1))
-
-    def peers(step):
-        for d in order:
-            step(d, at[d])
-
-    def send_random(a):
-        def step(d, peer):
-            for t in range(cap):
-                og[a, peer, t] = slot_term(a, sidx[peer, t]).astype(BF16)
-            out_copy(a, d, peer, me).start()
-
-        peers(step)
 
     on_part = (lambda f: f()) if stride == 1 else pl.when(lax.rem(me, stride) == 0)
     my_part = lax.div(me, jnp.int32(stride))
@@ -331,7 +365,11 @@
     def take_random(a):
         def step(d, peer):
             out_copy(a, d, peer, peer).wait_recv()
-            take(a, [og_in[a, peer, t].astype(F32) for t in range(cap)], [roff[peer, t] for t in range(cap)])
+            blocks = [og_in[a, peer, t].astype(F32) for t in range(cap)]
+            if a == 1:
+                corr_copy(d, peer, peer).wait_recv()
+                blocks = [x + correction(peer, t) for t, x in enumerate(blocks)]
+            take(a, blocks, [roff[peer, t] for t in range(cap)])
 
         peers(step)
 
@@ -345,7 +383,7 @@
             gall[n * count : (n + 1) * count, a].astype(F32).reshape(BLOCK, D) for n in range(GLOBAL)]
         take(a, blocks, [glob_ref[n] - me * nb for n in range(GLOBAL)])
 
-    send_random(1)
+    send_corrections()
     pairs(0, nb // 2, score_grad)
     send_global()
     send_random(0)
@@ -381,6 +419,7 @@
             copy.wait_send()
 
     parts_loop(lambda j: part_copy(j, j * stride, me).wait_send())
+    peers(lambda d, peer: corr_copy(d, peer, me).wait_send())
 
     @on_part
     def _():
@@ -393,8 +432,14 @@
 def store(*refs):
     count = (len(refs) - 2) // 3
     src, dst, buf = (refs[n * count : (n + 1) * count] for n in range(3))
-    loads = [pltpu.make_async_copy(src[n], buf[n], refs[-2].at[n]) for n in range(count)]
-    stores = [pltpu.make_async_copy(buf[n], dst[n], refs[-1].at[n]) for n in range(count)]
+    loads, stores = [], []
+    for n in range(count):
+        lead = src[n].shape[0]
+        pieces = 4 if lead % 4 == 0 else 1
+        for piece in range(pieces):
+            cut = pl.ds(piece * (lead // pieces), lead // pieces)
+            loads.append(pltpu.make_async_copy(src[n].at[cut], buf[n].at[cut], refs[-2].at[n, piece]))
+            stores.append(pltpu.make_async_copy(buf[n].at[cut], dst[n].at[cut], refs[-1].at[n, piece]))
     for copy in loads:
         copy.start()
     for load, copy in zip(loads, stores):
@@ -458,6 +503,10 @@
             dma((2, 2)), dma((2, 2)),
             dma((PARTS,)), dma((S,)),
             dma((S,)), dma((PARTS,)), dma((5,)),
+            pltpu.VMEM((nb, 16, BLOCK), BF16),
+            pltpu.VMEM((S, 16, D), BF16),
+            pltpu.VMEM((S, 16, D), BF16),
+            dma((S,)), dma((S,)),
         ],
         compiler_params=pltpu.CompilerParams(
             collective_id=0, has_side_effects=True, vmem_limit_bytes=VMEM),
@@ -470,7 +519,7 @@
         out_shape=results,
         in_specs=[hbm] * 5,
         out_specs=[hbm] * 5,
-        scratch_shapes=[pltpu.VMEM(x.shape, x.dtype) for x in results] + [dma((5,))] * 2,
+        scratch_shapes=[pltpu.VMEM(x.shape, x.dtype) for x in results] + [dma((5, 4))] * 2,
         compiler_params=pltpu.CompilerParams(vmem_limit_bytes=VMEM),
     )(*done)
     flat = lambda x: x.reshape(T, D)

time: 41 us -> 39.1 us (0.954)
  Pallas kernels: 40.2 us -> 38.3 us
    pallas_call x1, Pallas kernels: 38.2 us -> 36.1 us  [body(): pl.pallas_call(functools.partial(kernel, S, H, nb, D, cap), out_shape=res...]
where the time goes in v7:
time: 39.1 us; the launch traced here: 38.9 us
  Pallas kernels  38.3 us (98%)
  between operations  0.64 us (2%)
    pallas_call x1, Pallas kernels, body(): pl.pallas_call(functools.partial(kernel, S, H, nb, D, cap), out_shape=res...  36.1 us
    pallas_call x1, Pallas kernels, body(): pl.pallas_call(store, out_shape=results, in_specs=[hbm] * 5, out_specs=[h...  2.2 us

profile of v7, /device:TPU:0, one launch (start us, length us, event | category | flops | bytes accessed | tf_op | source)
XLA Modules:
  0.0 38.9 jit_solution(2785113396913215997)
XLA Ops:
  0.6 36.1 %shard_map.119 = (bf16[8,64,128]{2,1,0:T(8,128)(2,1)}, f32[1,512]{1,0:T(1,128)}, f32[8,64,128]{2,1,0:T(8,128)}, f32[8,64,128]{2,1,0:T(8,128)}, f32[8,64,128]{2,1,0:T(8,128)}) custom-call(bf16[8,64,128]{2,1,0:T(8,128)(2,1)} %bitcast.12, bf16[8,64,128]{2,1,0:T(8,128)(2,1)} %bitcast.13, bf16[8,64,128]{2,1,0:T(8,128)(2,1)} %bitcast.14, ...), custom_call_target="tpu_custom_call" | custom-call | tf_op jit(solution)/shard_map/pallas_call | solution.py:469
  36.7 2.2 %shard_map.120 = (bf16[8,64,128]{2,1,0:T(8,128)(2,1)}, f32[1,512]{1,0:T(1,128)}, f32[8,64,128]{2,1,0:T(8,128)}, f32[8,64,128]{2,1,0:T(8,128)}, f32[8,64,128]{2,1,0:T(8,128)}) custom-call(bf16[8,64,128]{2,1,0:T(8,128)(2,1)} %get-tuple-element.15.refs_0_, f32[1,512]{1,0:T(1,128)} %get-tuple-element.16.refs_1_, f32[8,64,128]{2,1,0:T(8,128)} %get-tuple-element.17.refs_2_, ...), custom_call_target="tpu_custom_call" | custom-call | tf_op jit(solution)/shard_map/pallas_call | solution.py:517
